TPU v7x, 128 devices: a whole 4x4x4 slice. The times are simulated.
128 devices in a mesh: dp: 2 (over z_hi), space: 64 (over z_lo, x, y, core).
Axes of the slice: x: 4, y: 4, z: 4 (z_hi: 2, z_lo: 2; z = z_hi * 2 + z_lo), core: 2. Of those that a mesh axis runs over, the one named last changes fastest.
Arguments:
- inputs: float32 [2, 32, 128, 128, 128], P('dp', None, 'space'), may hold values from -6 to 6
- preact: float32 [2, 32, 128, 128, 128], P('dp', None, 'space'), may hold values from -6 to 6
- cotangent: float32 [2, 32, 128, 128, 128], P('dp', None, 'space'), may hold values from -6 to 6
- spectral_weight: float32 [32, 1024, 2048], P(None, 'space'), may hold values from -3 to 3
- skip_weight: float32 [32, 32], replicated, may hold values from -1 to 1
Outputs:
- input_grad: float32 [2, 32, 128, 128, 128], P('dp', None, 'space')
- weight_grad: float32 [32, 1024, 2048], P('dp', 'space')
- skip_grad: float32 [32, 32], replicated
All inputs are finite; a program needn't handle non-finite values.
Results may differ from a plain program's by a relative error of at most 0.00016.
Values sent between devices are 32-bit elements; how exact they have to be, the bound alone decides.
No kernel may reach another device: no remote copies, remote signals or barrier semaphores. Data moves between devices by JAX's collectives and lax.ppermute only.
A program may use at most 128 MiB of HBM per device.

v0:
```python
import functools

import jax
import jax.numpy as jnp
import numpy as np
from jax import lax
from jax.experimental import pallas as pl
from jax.experimental.pallas import tpu as pltpu
from jax.sharding import PartitionSpec as P

N = 128
C = 32
MX = 32
MY = 64
MZ = 16
SPACE = 64
GROUPS = C // 2
JL = 16
NORM = float(N) ** (-1.5)
TANH_SCALE = 0.7978845608028654
CUBIC = 0.044715
F32 = jnp.float32
BF16 = jnp.bfloat16
LIMIT = 40 * 1024 * 1024


def signed(count):
    index = np.arange(count)
    return np.where(index < count // 2, index, index - count)


def angles(frequency):
    points = np.arange(N)
    return 2.0 * np.pi / N * np.mod(frequency[:, None] * points[None, :], N)


ANGLE_X = angles(signed(MX))
ANGLE_Y = angles(signed(MY))
ANGLE_Z = angles(np.arange(MZ))


def halves(table):
    table = np.asarray(table, np.float64)
    high = table.astype(np.float32).astype(BF16)
    low = (table - high.astype(np.float64)).astype(np.float32).astype(BF16)
    return high, low


def split(value):
    high = value.astype(BF16)
    return high, (value - high.astype(F32)).astype(BF16)


def dot(left, right):
    return jnp.dot(left, right, preferred_element_type=F32)


def z_tables():
    high, low = halves(np.concatenate([np.cos(ANGLE_Z).T, -np.sin(ANGLE_Z).T], 1))
    table = np.zeros((4, 2, N, 2, 4, 2 * MZ), BF16)
    for plane in range(4):
        table[plane, 0, :, 0, plane] = high
        table[plane, 1, :, 0, plane] = high
        table[plane, 0, :, 1, plane] = low
    return table.reshape(8 * N, 256)


def y_tables():
    high, low = halves(np.concatenate([np.cos(ANGLE_Y), -np.sin(ANGLE_Y)], 0))
    return np.concatenate([high, high, low], 1)


def x_tables():
    cos_x, sin_x = np.cos(ANGLE_X), np.sin(ANGLE_X)
    table = np.zeros((2, MX, 2, N))
    table[0, :, 0], table[0, :, 1] = cos_x, sin_x
    table[1, :, 0], table[1, :, 1] = -sin_x, cos_x
    table = table.reshape(2, 2, MX // 2, 2, SPACE, 2).transpose(1, 0, 2, 5, 3, 4) * NORM
    high, low = halves(table.reshape(2 * MX, 4 * SPACE))
    return np.concatenate([high, low], 0)


def back_x_tables():
    cos_x, sin_x = np.cos(ANGLE_X), np.sin(ANGLE_X)
    table = np.zeros((2, MX, 2, N))
    table[0, :, 0], table[0, :, 1] = cos_x, sin_x
    table[1, :, 0], table[1, :, 1] = -sin_x, cos_x
    table = table.reshape(2, 2, MX // 2, 2, SPACE, 2).transpose(5, 3, 4, 1, 0, 2) * NORM
    high, low = halves(table.reshape(4 * SPACE, 2 * MX))
    return np.concatenate([high, high, low], 1)


def back_y_tables():
    high, low = halves(np.concatenate([np.cos(ANGLE_Y).T, np.sin(ANGLE_Y).T], 1))
    return np.concatenate([high, high, low], 1)


def back_z_tables():
    high, low = halves(np.concatenate([np.cos(ANGLE_Z), -np.sin(ANGLE_Z)], 0))
    table = np.zeros((3, 4, 2 * MZ, 4, N), BF16)
    for plane in range(4):
        table[0, plane, :, plane] = high
        table[1, plane, :, plane] = high
        table[2, plane, :, plane] = low
    return table.reshape(3 * 128, 4 * N)


def one_hot(hits):
    return jnp.where(hits, 1.0, 0.0).astype(BF16)


def reorder_matrix():
    row = lax.broadcasted_iota(jnp.int32, (C * JL, C * JL), 0)
    column = lax.broadcasted_iota(jnp.int32, (C * JL, C * JL), 1)
    sent, j = row >> 4, row & (JL - 1)
    channel = ((sent >> 4) * 8 + (sent & 7)) * 2 + ((sent >> 3) & 1)
    return one_hot(column == j * C + channel)


def spread_matrix():
    row = lax.broadcasted_iota(jnp.int32, (2 * C, C * C), 0)
    column = lax.broadcasted_iota(jnp.int32, (2 * C, C * C), 1)
    return one_hot((row & (C - 1)) == (column >> 5))


def rows_table():
    return np.repeat(np.eye(C), 8, 0).astype(BF16)


def fold_table():
    table = np.zeros((2, GROUPS, 8, C), BF16)
    for inner in range(2):
        for group in range(GROUPS):
            table[inner, group, :, 2 * group + inner] = 1
    return table.reshape(256, C)


def gelu_slope(h):
    square = h * h
    t = jnp.tanh(h * (TANH_SCALE + (TANH_SCALE * CUBIC) * square))
    inner = h * (0.5 * TANH_SCALE + (1.5 * TANH_SCALE * CUBIC) * square)
    return (0.5 + 0.5 * t) + (1.0 - t * t) * inner


def lane_swap(value, first_sign):
    lanes = lax.broadcasted_iota(jnp.int32, value.shape, value.ndim - 1)
    up = pltpu.roll(value, 128 - MZ, value.ndim - 1)
    down = pltpu.roll(value, MZ, value.ndim - 1)
    return jnp.where((lanes & MZ) == 0, first_sign * up, -first_sign * down)


YB = 32
CHUNKS = N // YB
TILES = YB // 8


def chunk_copy(ref, buffer, sem, chunk):
    rows = pl.ds(YB * chunk, YB)
    copy = pltpu.make_async_copy(ref.at[0, :, :, rows, :], buffer.at[:, :, rows, :], sem)
    copy.start()
    return copy


def whole_copy(ref, buffer, sem):
    copy = pltpu.make_async_copy(ref, buffer, sem)
    copy.start()
    return copy


def spread_planes(value, highs, lows, tile):
    value = value.reshape(GROUPS, 2, 2, 8, N)
    for inner in range(2):
        for plane in range(2):
            high, low = split(value[:, inner, plane].reshape(GROUPS * 8, N))
            place = (tile, slice(128 * inner, 128 * inner + 128), slice(128 * plane, 128 * plane + 128))
            highs[place] = high
            lows[place] = low


def transform_z(highs, lows, ztab_ref, scratch, chunk):
    rows = []
    for tile in range(TILES * chunk, TILES * chunk + TILES):
        wide = []
        for inner in range(2):
            for plane in range(2):
                place = (tile, slice(128 * inner, 128 * inner + 128), slice(128 * plane, 128 * plane + 128))
                wide += [highs[place], lows[place]]
        rows.append(jnp.concatenate(wide, 1))
    out = dot(jnp.concatenate(rows, 0), ztab_ref[...])
    out = out[:, :128] + out[:, 128:]
    for tile in range(TILES):
        place = YB * chunk + 8 * tile
        scratch[:, place:place + 8, :] = out[128 * tile:128 * tile + 128].reshape(GROUPS, 8, 128)


def transform_y(scratch, ytab_ref, half, send_ref, offset):
    for pair in range(GROUPS // 2):
        wide = jnp.concatenate([scratch[2 * pair], scratch[2 * pair + 1]], 1)
        high, low = split(wide)
        out = dot(ytab_ref[...], jnp.concatenate([high, low, high], 0))
        for member in range(2):
            mine = out[:, 128 * member:128 * member + 128]
            half[2 * pair + member] = mine[:MY] + lane_swap(mine[MY:], -1.0)
    for jq in range(4):
        for group_set in range(2):
            block = half[8 * group_set:8 * group_set + 8, JL * jq:JL * jq + JL, :]
            turned = block.reshape(128, 128).T
            for r in range(8):
                row = offset + 8 * group_set + r
                send_ref[pl.ds(jq, MZ, stride=4), row, :] = turned[MZ * r:MZ * r + MZ]


def forward_kernel(
    pre_hbm, cot_hbm, inp_hbm, ztab_hbm, ytab_hbm, send_hbm,
    pre, cot, inp, ztab, ytab, g_high, g_low, i_high, i_low, g_lines, i_lines, half, send, sems, tab_sems, out_sems,
):
    copies = []
    for chunk in range(CHUNKS):
        copies.append([
            chunk_copy(ref, buffer, sems.at[chunk, k], chunk)
            for k, (ref, buffer) in enumerate(((inp_hbm, inp), (pre_hbm, pre), (cot_hbm, cot)))
        ])
        if chunk == 0:
            ztab_copy = whole_copy(ztab_hbm, ztab, tab_sems.at[0])
    ytab_copy = whole_copy(ytab_hbm, ytab, tab_sems.at[1])
    for chunk in range(CHUNKS):
        tiles = range(TILES * chunk, TILES * chunk + TILES)
        copies[chunk][0].wait()
        for tile in tiles:
            spread_planes(inp[:, :, 8 * tile:8 * tile + 8, :], i_high, i_low, tile)
        if chunk == 0:
            ztab_copy.wait()
        transform_z(i_high, i_low, ztab, i_lines, chunk)
        copies[chunk][1].wait()
        copies[chunk][2].wait()
        for tile in tiles:
            rows = slice(8 * tile, 8 * tile + 8)
            spread_planes(cot[:, :, rows, :] * gelu_slope(pre[:, :, rows, :]), g_high, g_low, tile)
        transform_z(g_high, g_low, ztab, g_lines, chunk)
    ytab_copy.wait()
    outs = []
    for k, lines in enumerate((g_lines, i_lines)):
        transform_y(lines, ytab, half.at[k], send, 16 * k)
        rows = pl.ds(16 * k, 16)
        outs.append(whole_copy(send.at[:, rows], send_hbm.at[:, rows], out_sems.at[k]))
    for copy in outs:
        copy.wait()


def in_vmem(count):
    return [pl.BlockSpec(memory_space=pltpu.VMEM) for _ in range(count)]


def vmem_spec():
    return pl.BlockSpec(memory_space=pltpu.VMEM)


def any_spec():
    return pl.BlockSpec(memory_space=pl.ANY)


FIELD = (C, 2, N, N)
HALF = (C // 2, 2, N, N)


PAIR = (N // 8, 256, 256)


def in_hbm(value):
    return pltpu.with_memory_space_constraint(value, pltpu.HBM)


def kept(value):
    return pltpu.with_memory_space_constraint(value, pltpu.VMEM)


def forward(preact, cotangent, inputs):
    ztab, ytab = jnp.asarray(z_tables()), jnp.asarray(y_tables())
    return pl.pallas_call(
        forward_kernel,
        in_specs=[any_spec()] * 5,
        out_specs=any_spec(),
        out_shape=pltpu.HBM((SPACE, FIRST, 128), F32),
        scratch_shapes=[pltpu.VMEM(FIELD, F32)] * 3 + [
            pltpu.VMEM(ztab.shape, BF16), pltpu.VMEM(ytab.shape, BF16),
        ] + [pltpu.VMEM(PAIR, BF16)] * 4 + [
            pltpu.VMEM((GROUPS, N, 128), F32), pltpu.VMEM((GROUPS, N, 128), F32),
            pltpu.VMEM((2, GROUPS, MY, 128), F32), pltpu.VMEM((SPACE, FIRST, 128), F32),
            pltpu.SemaphoreType.DMA((CHUNKS, 3)), pltpu.SemaphoreType.DMA((2,)), pltpu.SemaphoreType.DMA((2,)),
        ],
        compiler_params=pltpu.CompilerParams(vmem_limit_bytes=LIMIT),
        name="forward",
    )(in_hbm(preact), in_hbm(cotangent), in_hbm(inputs), in_hbm(ztab), in_hbm(ytab))


ACROSS = (((1,), (1,)), ((), ()))


def same_row():
    left = lax.broadcasted_iota(jnp.int32, (256, 256), 0) & 7
    right = lax.broadcasted_iota(jnp.int32, (256, 256), 1) & 7
    return left == right


def skip_kernel(
    pre_hbm, cot_hbm, inp_hbm, skip_ref, rows_ref, fold_ref, near, term_hbm, part_ref,
    pre, cot, inp, term, g_high, g_low, i_high, i_low, acc, sems, out_sems,
):
    copies = []
    for chunk in range(CHUNKS):
        copies.append([
            chunk_copy(ref, buffer, sems.at[chunk, k], chunk)
            for k, (ref, buffer) in enumerate(((inp_hbm, inp), (pre_hbm, pre), (cot_hbm, cot)))
        ])
    matrix = []
    for part in split(skip_ref[...]):
        wide = lax.dot_general(rows_ref[...], part, ACROSS, preferred_element_type=F32).astype(BF16)
        wide = lax.dot_general(wide, fold_ref[...], ACROSS, preferred_element_type=F32)
        matrix.append(jnp.where(same_row(), wide, 0.0).astype(BF16))
    matrix = jnp.concatenate(matrix, 0)
    outs = []
    for chunk in range(CHUNKS):
        for copy in copies[chunk]:
            copy.wait()
        for tile in range(TILES * chunk, TILES * chunk + TILES):
            rows = slice(8 * tile, 8 * tile + 8)
            spread_planes(inp[:, :, rows, :], i_high, i_low, tile)
            spread_planes(cot[:, :, rows, :] * gelu_slope(pre[:, :, rows, :]), g_high, g_low, tile)
            out = dot(matrix, g_high[tile])
            out = out[:256] + out[256:] + dot(matrix[:256], g_low[tile])
            for plane in range(2):
                value = out[:, 128 * plane:128 * plane + 128].reshape(C, 8, N)
                near[:, plane, rows, :] = value[:C // 2]
                term[:, plane, rows, :] = value[C // 2:]
            total = (
                lax.dot_general(g_high[tile], i_high[tile], ACROSS, preferred_element_type=F32)
                + lax.dot_general(g_low[tile], i_high[tile], ACROSS, preferred_element_type=F32)
                + lax.dot_general(g_high[tile], i_low[tile], ACROSS, preferred_element_type=F32)
            )
            if tile == 0:
                acc[...] = total
            else:
                acc[...] += total
        rows = pl.ds(YB * chunk, YB)
        outs.append(whole_copy(term.at[:, :, rows, :], term_hbm.at[:, :, rows, :], out_sems.at[chunk]))
    diagonal = jnp.where(same_row(), acc[...], 0.0) * NORM
    fold = fold_ref[...].astype(F32)
    folded = jnp.dot(diagonal, fold, preferred_element_type=F32, precision=lax.Precision.HIGHEST)
    summed = lax.dot_general(
        fold, folded, (((0,), (0,)), ((), ())), preferred_element_type=F32,
        precision=lax.Precision.HIGHEST,
    )
    part_ref[...] = jnp.concatenate([summed[8 * q:8 * q + 8, :] for q in range(4)], 1)
    for copy in outs:
        copy.wait()


def skip_products(preact, cotangent, inputs, skip_weight):
    return pl.pallas_call(
        skip_kernel,
        in_specs=[any_spec()] * 3 + in_vmem(3),
        out_specs=[vmem_spec(), any_spec(), vmem_spec()],
        out_shape=[pltpu.VMEM(HALF, F32), pltpu.HBM(HALF, F32), jax.ShapeDtypeStruct((8, 128), F32)],
        scratch_shapes=[pltpu.VMEM(FIELD, F32)] * 3 + [pltpu.VMEM(HALF, F32)] + [pltpu.VMEM(PAIR, BF16)] * 4 + [
            pltpu.VMEM((256, 256), F32),
            pltpu.SemaphoreType.DMA((CHUNKS, 3)), pltpu.SemaphoreType.DMA((CHUNKS,)),
        ],
        compiler_params=pltpu.CompilerParams(vmem_limit_bytes=LIMIT),
        name="skip_products",
    )(in_hbm(preact), in_hbm(cotangent), in_hbm(inputs), skip_weight, rows_table(), fold_table())


FIRST = 32
SECOND = 24


def transform_x(recv_ref, offset, xtab_ref, reorder):
    blocks = []
    for q in range(4):
        column = [recv_ref[pl.ds(offset + 4 * q + r, SPACE, stride=FIRST), :] for r in range(4)]
        blocks.append(jnp.concatenate(column, 0))
    high, low = split(jnp.concatenate(blocks, 1))
    out = dot(xtab_ref[...], high)
    spectrum = out[:2 * MX] + out[2 * MX:] + dot(xtab_ref[:2 * MX], low)
    out = dot(jnp.concatenate(split(spectrum), 0), reorder)
    return out[:2 * MX] + out[2 * MX:]


def to_rows(spectrum, scratch):
    for j in range(JL):
        scratch[:, j, :] = spectrum[:, C * j:C * j + C]


def spectrum_kernel(dp_ref, recv_ref, xtab_ref, part_ref, w_hbm, spec_ref, mine_ref, theirs_ref, w_ref, sem):
    early = whole_copy(w_hbm.at[pl.ds(0, MX // 2)], w_ref, sem.at[0])
    reorder = reorder_matrix()
    first = dp_ref[0] == 0
    for k in range(2):
        spectrum = transform_x(recv_ref, 16 * k, xtab_ref, reorder)
        if k == 0:
            spec_ref[...] = spectrum
        mine_ref[MX * k:MX * k + MX, :] = jnp.where(first, spectrum[:MX], spectrum[MX:])
        theirs_ref[MX * k:MX * k + MX, :] = jnp.where(first, spectrum[MX:], spectrum[:MX])
    early.wait()


def spectra(dp, received, part, weights):
    return pl.pallas_call(
        spectrum_kernel,
        in_specs=[pl.BlockSpec(memory_space=pltpu.SMEM)] + in_vmem(2) + [any_spec()] * 2,
        out_specs=in_vmem(4),
        out_shape=[
            jax.ShapeDtypeStruct((2 * MX, JL * C), F32),
            jax.ShapeDtypeStruct((2 * MX, JL * C), F32),
            jax.ShapeDtypeStruct((2 * MX, JL * C), F32),
            pltpu.VMEM((MX // 2, JL, 2 * C * C), F32),
        ],
        scratch_shapes=[pltpu.SemaphoreType.DMA((1,))],
        compiler_params=pltpu.CompilerParams(vmem_limit_bytes=LIMIT),
        name="spectra",
    )(dp, received, x_tables(), part, in_hbm(weights))


WB = 8


def dual_kernel(
    spec_ref, early_ref, w_hbm, dual, late_ref, spec, wide, sems,
):
    copies = []
    for block in range(MX // WB // 2):
        rows = pl.ds(WB * block, WB)
        copies.append(whole_copy(w_hbm.at[pl.ds(MX // 2 + WB * block, WB)], late_ref.at[rows], sems.at[block]))
    spread = spread_matrix()
    to_rows(spec_ref[...], spec)
    for block in range(MX // WB):
        start = 32 * (WB * block // 16) + WB * block % 16
        both = jnp.concatenate([spec[start:start + WB], spec[start + 16:start + 16 + WB]], 0)
        high, low = split(both.reshape(2 * WB * JL, C))
        wide[block % 2] = dot(jnp.concatenate([high, low], 1), spread)
        w_ref = early_ref if block < MX // WB // 2 else late_ref
        if block >= MX // WB // 2:
            copies[block - MX // WB // 2].wait()
        for local in range(WB):
            total_real, total_imag = None, None
            for tile in range(8):
                lanes = slice(128 * tile, 128 * tile + 128)
                real = wide[block % 2, JL * local:JL * local + JL, lanes]
                imag = wide[block % 2, JL * (WB + local):JL * (WB + local) + JL, lanes]
                m = (WB * block + local) % (MX // 2)
                w_real = w_ref[m, :, lanes]
                w_imag = w_ref[m, :, 1024 + 128 * tile:1024 + 128 * tile + 128]
                out_real = w_real * real + w_imag * imag
                out_imag = w_real * imag - w_imag * real
                total_real = out_real if tile == 0 else total_real + out_real
                total_imag = out_imag if tile == 0 else total_imag + out_imag
            for total, place in ((total_real, start + local), (total_imag, start + 16 + local)):
                total = total + pltpu.roll(total, 64, 1)
                dual[place] = total + pltpu.roll(total, 32, 1)


def lines_kernel(dual, part_ref, other_ref, back_ref, got_ref, send_hbm, send, sems):
    skip = part_ref[...] + other_ref[...]
    for dest in range(SPACE):
        send[dest, 16:] = skip
    rows = pl.ds(16, 8)
    copies = [whole_copy(send.at[:, rows], send_hbm.at[:, rows], sems.at[2])]
    reorder = reorder_matrix()
    lanes = lax.broadcasted_iota(jnp.int32, (2 * MX, 128), 1) // C
    blocks = []
    for j4 in range(4):
        block = dual[:, 4 * j4, :]
        for k in range(1, 4):
            block = jnp.where(lanes == k, dual[:, 4 * j4 + k, :], block)
        blocks.append(block)
    both = jnp.concatenate(split(jnp.concatenate(blocks, 1)), 0)
    ordered = lax.dot_general(both, reorder, ACROSS, preferred_element_type=F32)
    high, low = split(ordered[:2 * MX] + ordered[2 * MX:])
    out = dot(back_ref[...], jnp.concatenate([high, low, high], 0))
    for half in range(2):
        for q in (2 * half, 2 * half + 1):
            for r in range(4):
                send[:, 4 * q + r, :] = out[SPACE * r:SPACE * r + SPACE, 128 * q:128 * q + 128]
        rows = pl.ds(8 * half, 8)
        copies.append(whole_copy(send.at[:, rows], send_hbm.at[:, rows], sems.at[half]))
    for copy in copies:
        copy.wait()


def dual_rows(spectrum, early, weights):
    return pl.pallas_call(
        dual_kernel,
        in_specs=in_vmem(2) + [any_spec()],
        out_specs=vmem_spec(),
        out_shape=jax.ShapeDtypeStruct((2 * MX, JL, 128), F32),
        scratch_shapes=[
            pltpu.VMEM((MX // 2, JL, 2 * C * C), F32), pltpu.VMEM((2 * MX, JL, C), F32),
            pltpu.VMEM((2, 2 * WB * JL, C * C), F32),
            pltpu.SemaphoreType.DMA((MX // WB // 2,)),
        ],
        compiler_params=pltpu.CompilerParams(vmem_limit_bytes=LIMIT),
        name="dual_rows",
    )(spectrum, kept(early), in_hbm(weights))


def dual_lines(dual, part, other, got):
    return pl.pallas_call(
        lines_kernel,
        in_specs=in_vmem(4) + [any_spec()],
        out_specs=any_spec(),
        out_shape=pltpu.HBM((SPACE, SECOND, 128), F32),
        scratch_shapes=[pltpu.VMEM((SPACE, SECOND, 128), F32), pltpu.SemaphoreType.DMA((3,))],
        compiler_params=pltpu.CompilerParams(vmem_limit_bytes=LIMIT),
        name="dual_lines",
    )(dual, part, other, back_x_tables(), got)


MB = 4


def weight_kernel(
    mine_ref, got_ref, out_hbm, grads, fields, wide, out, sems,
):
    spread = spread_matrix()
    to_rows(mine_ref[:MX], grads.at[0])
    to_rows(got_ref[:MX], grads.at[1])
    for b, value in enumerate((mine_ref[MX:], got_ref[MX:])):
        for j in range(JL):
            piece = value[:, C * j:C * j + C]
            fields[b, :, j, :] = jnp.concatenate([piece] * 4, 1)
    copies = []
    for block in range(16 // MB):
        rows = jnp.concatenate(
            [grads[b, 16 * s + MB * block:16 * s + MB * block + MB] for b in range(2) for s in range(2)], 0
        )
        high, low = split(rows.reshape(4 * MB * JL, C))
        wide[...] = dot(jnp.concatenate([high, low], 1), spread)
        for local in range(MB):
            m = MB * block + local
            f = [fields[b, m + 16 * s] for b in range(2) for s in range(2)]
            for tile in range(8):
                lanes = slice(128 * tile, 128 * tile + 128)
                g = [wide[JL * (MB * q + local):JL * (MB * q + local) + JL, lanes] for q in range(4)]
                out[m, :, lanes] = g[0] * f[0] + g[1] * f[1] + g[2] * f[2] + g[3] * f[3]
                out[m, :, 1024 + 128 * tile:1024 + 128 * tile + 128] = (
                    g[1] * f[0] - g[0] * f[1] + g[3] * f[2] - g[2] * f[3]
                )
        rows = pl.ds(MB * block, MB)
        copy = pltpu.make_async_copy(out.at[rows], out_hbm.at[rows], sems.at[block])
        copy.start()
        copies.append(copy)
    for copy in copies:
        copy.wait()


def weight_gradient(mine, got):
    return pl.pallas_call(
        weight_kernel,
        in_specs=in_vmem(2),
        out_specs=any_spec(),
        out_shape=pltpu.HBM((16, JL, 2 * C * C), F32),
        scratch_shapes=[
            pltpu.VMEM((2, MX, JL, C), F32), pltpu.VMEM((2, MX, JL, 128), F32),
            pltpu.VMEM((4 * MB * JL, C * C), F32), pltpu.VMEM((16, JL, 2 * C * C), F32),
            pltpu.SemaphoreType.DMA((16 // MB,)),
        ],
        compiler_params=pltpu.CompilerParams(vmem_limit_bytes=LIMIT),
        name="weight_gradient",
    )(mine, got)


GB = 4


def backward_kernel(
    recv_ref, near, term_hbm, ytab_ref, ztab_hbm, out_hbm, skip_ref, term, ztab, out, half, lhs, sems, out_sems,
):
    ztab_copy = whole_copy(ztab_hbm, ztab, sems.at[0])
    term_copy = whole_copy(term_hbm, term, sems.at[1])
    for jq in range(4):
        for group_set in range(2):
            rows = [recv_ref[pl.ds(jq * SECOND + 8 * group_set + r, MZ, stride=4 * SECOND), :] for r in range(8)]
            turned = jnp.concatenate(rows, 0).T
            half[8 * group_set:8 * group_set + 8, JL * jq:JL * jq + JL, :] = turned.reshape(8, JL, 128)
    total = recv_ref[16:24, :]
    for source in range(1, SPACE):
        total = total + recv_ref[SECOND * source + 16:SECOND * source + 24, :]
    for q in range(4):
        skip_ref[8 * q:8 * q + 8, :] = total[:, C * q:C * q + C]
    outs = []
    for block in range(GROUPS // GB):
        for pair in range(GB // 2):
            both = []
            for member in range(2):
                value = half[GB * block + 2 * pair + member]
                both.append(jnp.concatenate([value, lane_swap(value, -1.0)], 0))
            high, low = split(jnp.concatenate(both, 1))
            lines = dot(ytab_ref[...], jnp.concatenate([high, low, high], 0))
            for member in range(2):
                high, low = split(lines[:, 128 * member:128 * member + 128])
                rows = slice(128 * (2 * pair + member), 128 * (2 * pair + member) + 128)
                lhs[rows, :128] = high
                lhs[rows, 128:256] = low
                lhs[rows, 256:] = high
        if block == 0:
            ztab_copy.wait()
        value = dot(lhs[...], ztab[...])
        if 2 * block == GROUPS // GB:
            term_copy.wait()
        for group in range(GB):
            for inner in range(2):
                for plane in range(2):
                    lane = 128 * (2 * inner + plane)
                    place = 2 * (GB * block + group) + inner
                    extra = near[place, plane] if place < C // 2 else term[place - C // 2, plane]
                    out[place, plane] = value[128 * group:128 * group + 128, lane:lane + 128] + extra
        rows = pl.ds(2 * GB * block, 2 * GB)
        copy = pltpu.make_async_copy(out.at[rows], out_hbm.at[0, rows], out_sems.at[block])
        copy.start()
        outs.append(copy)
    for copy in outs:
        copy.wait()


def backward(received, near, term):
    ztab = jnp.asarray(back_z_tables())
    return pl.pallas_call(
        backward_kernel,
        in_specs=in_vmem(2) + [any_spec(), vmem_spec(), any_spec()],
        out_specs=[any_spec(), vmem_spec()],
        out_shape=[pltpu.HBM((1, C, 2, N, N), F32), jax.ShapeDtypeStruct((C, C), F32)],
        scratch_shapes=[
            pltpu.VMEM(HALF, F32), pltpu.VMEM(ztab.shape, BF16), pltpu.VMEM(FIELD, F32),
            pltpu.VMEM((GROUPS, MY, 128), F32), pltpu.VMEM((GB * 128, 384), BF16),
            pltpu.SemaphoreType.DMA((2,)), pltpu.SemaphoreType.DMA((GROUPS // GB,)),
        ],
        compiler_params=pltpu.CompilerParams(vmem_limit_bytes=LIMIT),
        name="backward",
    )(received, kept(near), in_hbm(term), back_y_tables(), in_hbm(ztab))


def exchange(sent, rows):
    swapped = lax.all_to_all(sent, "space", 0, 0, tiled=True)
    return swapped.reshape(SPACE * rows, 128)


def body(inputs, preact, cotangent, spectral_weight, skip_weight):
    dp = lax.axis_index("dp").astype(jnp.int32).reshape(1)
    pair = [(0, 1), (1, 0)]
    received = exchange(forward(preact, cotangent, inputs), FIRST)
    near, term, part = skip_products(preact, cotangent, inputs, skip_weight)
    other = lax.ppermute(part, "dp", pair)
    spectrum, mine, theirs, early = spectra(dp, received, other, spectral_weight)
    got = lax.ppermute(theirs, "dp", pair)
    dual = dual_rows(spectrum, early, spectral_weight)
    got_dual = exchange(dual_lines(dual, part, other, got), SECOND)
    weight_grad = weight_gradient(mine, got)
    input_grad, skip_grad = backward(got_dual, near, term)
    return input_grad, weight_grad, skip_grad


def solution(mesh):
    in_specs = (
        P("dp", None, "space", None, None),
        P("dp", None, "space", None, None),
        P("dp", None, "space", None, None),
        P(None, "space", None),
        P(),
    )
    out_specs = (P("dp", None, "space", None, None), P("dp", "space", None), P())
    return jax.shard_map(body, mesh=mesh, in_specs=in_specs, out_specs=out_specs, check_vma=False)
```

profile of v0, /device:TPU:1, one launch (start us, length us, event | category | flops | bytes accessed | tf_op | source)
XLA Modules:
  0.0 79.5 jit_solution(2945945436493362646)
XLA Ops:
  0.6 0.0 copy-start.3
  0.6 0.0 copy-start.4
  0.7 0.0 copy-start.5
  0.7 13.6 %forward.1 = f32[64,32,128]{2,1,0:T(8,128)} custom-call(f32[1,32,2,128,128]{4,3,2,1,0:T(8,128)} %pre_hbm.3, f32[1,32,2,128,128]{4,3,2,1,0:T(8,128)} %cot_hbm.3, f32[1,32,2,128,128]{4,3,2,1,0:T(8,128)} %inp_hbm.3, bf16[1024,256]{1,0:T(8,128)(2,1)} %constant.22.clone.ztab_hbm, bf16[128,384]{1,0:T(8,128)(2,1)} %constant.23.clone.ytab_hbm), custom_call_target="tpu_custom_call" | custom-call | tf_op jit(solution)/shard_map/forward/pallas_call | solution.py:279
  14.2 10.4 %all-to-all-start = ((f32[64,32,128]{2,1,0:T(8,128)}), f32[64,32,128]{2,1,0:T(8,128)S(1)}, u32[]{:S(2)}, u32[]{:S(2)}) async-start(f32[64,32,128]{2,1,0:T(8,128)} %forward.1), calls=%async_computation | async-start | bytes 2097152 | tf_op jit(solution)/shard_map/all_to_all | solution.py:643
  24.6 0.0 copy-done.3
  24.6 0.0 copy-done.4
  24.6 0.0 copy-done.5
  24.6 0.0 copy-start.2
  24.6 8.9 %skip_products.1 = (f32[16,2,128,128]{3,2,1,0:T(8,128)S(1)}, f32[16,2,128,128]{3,2,1,0:T(8,128)}, f32[8,128]{1,0:T(8,128)S(1)}) custom-call(f32[1,32,2,128,128]{4,3,2,1,0:T(8,128)} %pre_hbm.3, f32[1,32,2,128,128]{4,3,2,1,0:T(8,128)} %cot_hbm.3, f32[1,32,2,128,128]{4,3,2,1,0:T(8,128)} %inp_hbm.3, f32[32,32]{1,0:T(8,128)S(1)} %copy-done.5, ...), custom_call_target="tpu_custom_call" | custom-call | tf_op jit(solution)/shard_map/skip_products/pallas_call | solution.py:359
  33.6 3.4 %collective-permute-start = (f32[8,128]{1,0:T(8,128)S(1)}, f32[8,128]{1,0:T(8,128)S(1)}, u32[]{:S(2)}, u32[]{:S(2)}) collective-permute-start(f32[8,128]{1,0:T(8,128)S(1)} %get-tuple-element.12.part_ref), channel_id=1, source_target_pairs={{0,64},{64,0},{1,65},{65,1},{2,66},{66,2},{3,67},{67,3},{4,68},{68... | collective-permute-start | bytes 12296 | tf_op jit(solution)/shard_map/ppermute | solution.py:652
  37.0 1.7 %collective-permute-done.part_ref.other_ref = f32[8,128]{1,0:T(8,128)S(1)} collective-permute-done((f32[8,128]{1,0:T(8,128)S(1)}, f32[8,128]{1,0:T(8,128)S(1)}, u32[]{:S(2)}, u32[]{:S(2)}) %collective-permute-start) | collective-permute-done | bytes 4128 | tf_op jit(solution)/shard_map/ppermute | solution.py:652
  38.7 3.3 %all-to-all-done = f32[64,32,128]{2,1,0:T(8,128)S(1)} async-done(((f32[64,32,128]{2,1,0:T(8,128)}), f32[64,32,128]{2,1,0:T(8,128)S(1)}, u32[]{:S(2)}, u32[]{:S(2)}) %all-to-all-start) | async-done | bytes 1048608 | tf_op jit(solution)/shard_map/all_to_all | solution.py:643
  41.9 0.0 copy-done.2
  41.9 1.6 %spectra.1 = (f32[64,512]{1,0:T(8,128)S(1)}, f32[64,512]{1,0:T(8,128)S(1)}, f32[64,512]{1,0:T(8,128)S(1)}, f32[16,16,2048]{2,1,0:T(8,128)S(1)}) custom-call(s32[1]{0:T(128)} %bitcast.dp_ref, f32[2048,128]{1,0:T(8,128)S(1)} %bitcast.3, bf16[128,256]{1,0:T(8,128)(2,1)S(1)} %copy-done.2, f32[8,128]{1,0:T(8,128)S(1)} %collective-permute-done.part_ref.other_ref, ...), custom_call_target="tpu_custom_call" | custom-call | tf_op jit(solution)/shard_map/spectra/pallas_call | solution.py:408
  43.6 0.0 copy-start
  43.6 3.4 %collective-permute-start.1 = (f32[64,512]{1,0:T(8,128)S(1)}, f32[64,512]{1,0:T(8,128)S(1)}, u32[]{:S(2)}, u32[]{:S(2)}) collective-permute-start(f32[64,512]{1,0:T(8,128)S(1)} %get-tuple-element.15), channel_id=1, source_target_pairs={{0,64},{64,0},{1,65},{65,1},{2,66},{66,2},{3,67},{67,3},{4,68},{68... | collective-permute-start | bytes 393224 | tf_op jit(solution)/shard_map/ppermute | solution.py:654
  46.9 3.4 %dual_rows.1.dual = f32[64,16,128]{2,1,0:T(8,128)S(1)} custom-call(f32[64,512]{1,0:T(8,128)S(1)} %get-tuple-element.13.spec_ref, f32[16,16,2048]{2,1,0:T(8,128)S(1)} %get-tuple-element.14.early_ref, f32[32,16,2048]{2,1,0:T(8,128)} %w_hbm.3), custom_call_target="tpu_custom_call" | custom-call | tf_op jit(solution)/shard_map/dual_rows/pallas_call | solution.py:491
  50.3 0.0 copy-start.1
  50.4 0.0 collective-permute-done.1.got_ref
  50.4 0.0 copy-done
  50.4 2.0 %dual_lines.1 = f32[64,24,128]{2,1,0:T(8,128)} custom-call(f32[64,16,128]{2,1,0:T(8,128)S(1)} %dual_rows.1.dual, f32[8,128]{1,0:T(8,128)S(1)} %get-tuple-element.12.part_ref, f32[8,128]{1,0:T(8,128)S(1)} %collective-permute-done.part_ref.other_ref, bf16[256,192]{1,0:T(8,128)(2,1)S(1)} %copy-done, f32[64,512]{1,0:T(8,128)S(1)} %collective-permute-done.1.got_ref), custom_call_target="tpu_custom_call" | custom-call | tf_op jit(solution)/shard_map/dual_lines/pallas_call | solution.py:507
  52.4 7.2 %all-to-all-start.1 = ((f32[64,24,128]{2,1,0:T(8,128)}), f32[64,24,128]{2,1,0:T(8,128)S(1)}, u32[]{:S(2)}, u32[]{:S(2)}) async-start(f32[64,24,128]{2,1,0:T(8,128)} %dual_lines.1), calls=%async_computation.1 | async-start | bytes 1572864 | tf_op jit(solution)/shard_map/all_to_all | solution.py:643
  59.6 3.5 %weight_gradient.1 = f32[16,16,2048]{2,1,0:T(8,128)} custom-call(f32[64,512]{1,0:T(8,128)S(1)} %get-tuple-element.19.mine_ref, f32[64,512]{1,0:T(8,128)S(1)} %collective-permute-done.1.got_ref), custom_call_target="tpu_custom_call" | custom-call | tf_op jit(solution)/shard_map/weight_gradient/pallas_call | solution.py:557
  63.1 11.2 %all-to-all-done.1 = f32[64,24,128]{2,1,0:T(8,128)S(1)} async-done(((f32[64,24,128]{2,1,0:T(8,128)}), f32[64,24,128]{2,1,0:T(8,128)S(1)}, u32[]{:S(2)}, u32[]{:S(2)}) %all-to-all-start.1) | async-done | bytes 786464 | tf_op jit(solution)/shard_map/all_to_all | solution.py:643
  74.3 0.0 copy-done.1
  74.3 5.1 %backward.1 = (f32[1,32,2,128,128]{4,3,2,1,0:T(8,128)}, f32[32,32]{1,0:T(8,128)}) custom-call(f32[1536,128]{1,0:T(8,128)S(1)} %bitcast.4, f32[16,2,128,128]{3,2,1,0:T(8,128)S(1)} %get-tuple-element.16.near, f32[16,2,128,128]{3,2,1,0:T(8,128)} %get-tuple-element.17.term_hbm, bf16[128,384]{1,0:T(8,128)(2,1)S(1)} %copy-done.1, ...), custom_call_target="tpu_custom_call" | custom-call | tf_op jit(solution)/shard_map/backward/pallas_call | solution.py:627
Async XLA Ops:
  0.6 24.0 %copy-start.3 = (bf16[256,32]{1,0:T(8,128)(2,1)S(1)}, bf16[256,32]{1,0:T(8,128)(2,1)}, u32[]{:S(2)}) copy-start(bf16[256,32]{1,0:T(8,128)(2,1)} %constant.25.clone.fold_ref) | copy-start | bytes 49156
  0.6 24.0 %copy-start.4 = (bf16[256,32]{1,0:T(8,128)(2,1)S(1)}, bf16[256,32]{1,0:T(8,128)(2,1)}, u32[]{:S(2)}) copy-start(bf16[256,32]{1,0:T(8,128)(2,1)} %constant.24.clone.rows_ref) | copy-start | bytes 49156
  0.7 24.0 %copy-start.5 = (f32[32,32]{1,0:T(8,128)S(1)}, f32[32,32]{1,0:T(8,128)}, u32[]{:S(2)}) copy-start(f32[32,32]{1,0:T(8,128)} %skip_ref.1) | copy-start | bytes 12292
  14.2 27.7 %all-to-all-start = ((f32[64,32,128]{2,1,0:T(8,128)}), f32[64,32,128]{2,1,0:T(8,128)S(1)}, u32[]{:S(2)}, u32[]{:S(2)}) async-start(f32[64,32,128]{2,1,0:T(8,128)} %forward.1), calls=%async_computation | async-start | bytes 2097152 | tf_op jit(solution)/shard_map/all_to_all | solution.py:643
  24.6 17.3 %copy-start.2 = (bf16[128,256]{1,0:T(8,128)(2,1)S(1)}, bf16[128,256]{1,0:T(8,128)(2,1)}, u32[]{:S(2)}) copy-start(bf16[128,256]{1,0:T(8,128)(2,1)} %constant.26.clone.xtab_ref) | copy-start | bytes 196612
  33.6 5.1 %collective-permute-start = (f32[8,128]{1,0:T(8,128)S(1)}, f32[8,128]{1,0:T(8,128)S(1)}, u32[]{:S(2)}, u32[]{:S(2)}) collective-permute-start(f32[8,128]{1,0:T(8,128)S(1)} %get-tuple-element.12.part_ref), channel_id=1, source_target_pairs={{0,64},{64,0},{1,65},{65,1},{2,66},{66,2},{3,67},{67,3},{4,68},{68... | collective-permute-start | bytes 12296 | tf_op jit(solution)/shard_map/ppermute | solution.py:652
  43.6 6.8 %copy-start = (bf16[256,192]{1,0:T(8,128)(2,1)S(1)}, bf16[256,192]{1,0:T(8,128)(2,1)}, u32[]{:S(2)}) copy-start(bf16[256,192]{1,0:T(8,128)(2,1)} %constant.27.clone.back_ref) | copy-start | bytes 294916
  43.6 6.8 %collective-permute-start.1 = (f32[64,512]{1,0:T(8,128)S(1)}, f32[64,512]{1,0:T(8,128)S(1)}, u32[]{:S(2)}, u32[]{:S(2)}) collective-permute-start(f32[64,512]{1,0:T(8,128)S(1)} %get-tuple-element.15), channel_id=1, source_target_pairs={{0,64},{64,0},{1,65},{65,1},{2,66},{66,2},{3,67},{67,3},{4,68},{68... | collective-permute-start | bytes 393224 | tf_op jit(solution)/shard_map/ppermute | solution.py:654
  50.3 23.9 %copy-start.1 = (bf16[128,384]{1,0:T(8,128)(2,1)S(1)}, bf16[128,384]{1,0:T(8,128)(2,1)}, u32[]{:S(2)}) copy-start(bf16[128,384]{1,0:T(8,128)(2,1)} %constant.29.clone.ytab_ref) | copy-start | bytes 294916
  52.4 21.8 %all-to-all-start.1 = ((f32[64,24,128]{2,1,0:T(8,128)}), f32[64,24,128]{2,1,0:T(8,128)S(1)}, u32[]{:S(2)}, u32[]{:S(2)}) async-start(f32[64,24,128]{2,1,0:T(8,128)} %dual_lines.1), calls=%async_computation.1 | async-start | bytes 1572864 | tf_op jit(solution)/shard_map/all_to_all | solution.py:643
where the time goes:
time: 79.9 us; the launch traced here: 79.5 us
  Pallas kernels  38.1 us (48%)
  starting transfers between devices  24.3 us (30%)
  waiting for transfers between devices  16.1 us (20%)
  between operations  0.96 us (1%)
    all_to_all x2, starting transfers between devices, exchange(): swapped = lax.all_to_all(sent, 'space', 0, 0, tiled=True)  17.5 us
    all_to_all x2, waiting for transfers between devices, exchange(): swapped = lax.all_to_all(sent, 'space', 0, 0, tiled=True)  14.4 us
    pallas_call x1, Pallas kernels, forward(): pl.pallas_call(forward_kernel, in_specs=[any_spec()] * 5, out_specs=any_s...  13.6 us
    pallas_call x1, Pallas kernels, skip_products(): pl.pallas_call(skip_kernel, in_specs=[any_spec()] * 3 + in_vmem(3), out_s...  8.93 us
    pallas_call x1, Pallas kernels, backward(): pl.pallas_call(backward_kernel, in_specs=in_vmem(2) + [any_spec(), vmem_s...  5.07 us
    pallas_call x1, Pallas kernels, weight_gradient(): pl.pallas_call(weight_kernel, in_specs=in_vmem(2), out_specs=any_spec(),...  3.51 us
    pallas_call x1, Pallas kernels, dual_rows(): pl.pallas_call(dual_kernel, in_specs=in_vmem(2) + [any_spec()], out_specs...  3.39 us
    ppermute x1, starting transfers between devices, body(): other = lax.ppermute(part, 'dp', pair)  3.38 us
  transfers between devices with their start and end apart: 4, of which 3 were waited for; matrix products, arithmetic and copies ran while one was open for 0% of the time, Pallas kernels for 20%

commit v1 on v0

v1 whole, which is shorter than its diff:
```python
import functools

import jax
import jax.numpy as jnp
import numpy as np
from jax import lax
from jax.experimental import pallas as pl
from jax.experimental.pallas import tpu as pltpu
from jax.sharding import PartitionSpec as P

N = 128
C = 32
MX = 32
MY = 64
MZ = 16
SPACE = 64
GROUPS = C // 2
JL = 16
NORM = float(N) ** (-1.5)
TANH_SCALE = 0.7978845608028654
CUBIC = 0.044715
F32 = jnp.float32
BF16 = jnp.bfloat16
LIMIT = 40 * 1024 * 1024


def signed(count):
    index = np.arange(count)
    return np.where(index < count // 2, index, index - count)


def angles(frequency):
    points = np.arange(N)
    return 2.0 * np.pi / N * np.mod(frequency[:, None] * points[None, :], N)


ANGLE_X = angles(signed(MX))
ANGLE_Y = angles(signed(MY))
ANGLE_Z = angles(np.arange(MZ))


def halves(table):
    table = np.asarray(table, np.float64)
    high = table.astype(np.float32).astype(BF16)
    low = (table - high.astype(np.float64)).astype(np.float32).astype(BF16)
    return high, low


def split(value):
    high = value.astype(BF16)
    return high, (value - high.astype(F32)).astype(BF16)


def dot(left, right):
    return jnp.dot(left, right, preferred_element_type=F32)


def z_tables():
    high, low = halves(np.concatenate([np.cos(ANGLE_Z).T, -np.sin(ANGLE_Z).T], 1))
    table = np.zeros((4, 2, N, 2, 4, 2 * MZ), BF16)
    for plane in range(4):
        table[plane, 0, :, 0, plane] = high
        table[plane, 1, :, 0, plane] = high
        table[plane, 0, :, 1, plane] = low
    return table.reshape(8 * N, 256)


def y_tables():
    high, low = halves(np.concatenate([np.cos(ANGLE_Y), -np.sin(ANGLE_Y)], 0))
    return np.concatenate([high, high, low], 1)


def x_tables():
    cos_x, sin_x = np.cos(ANGLE_X), np.sin(ANGLE_X)
    table = np.zeros((2, MX, 2, N))
    table[0, :, 0], table[0, :, 1] = cos_x, sin_x
    table[1, :, 0], table[1, :, 1] = -sin_x, cos_x
    table = table.reshape(2, 2, MX // 2, 2, SPACE, 2).transpose(1, 0, 2, 5, 3, 4) * NORM
    high, low = halves(table.reshape(2 * MX, 4 * SPACE))
    return np.concatenate([high, low], 0)


def back_x_tables():
    cos_x, sin_x = np.cos(ANGLE_X), np.sin(ANGLE_X)
    table = np.zeros((2, MX, 2, N))
    table[0, :, 0], table[0, :, 1] = cos_x, sin_x
    table[1, :, 0], table[1, :, 1] = -sin_x, cos_x
    table = table.reshape(2, 2, MX // 2, 2, SPACE, 2).transpose(5, 3, 4, 1, 0, 2) * NORM
    high, low = halves(table.reshape(4 * SPACE, 2 * MX))
    return np.concatenate([high, high, low], 1)


def back_y_tables():
    high, low = halves(np.concatenate([np.cos(ANGLE_Y).T, np.sin(ANGLE_Y).T], 1))
    return np.concatenate([high, high, low], 1)


def back_z_tables():
    high, low = halves(np.concatenate([np.cos(ANGLE_Z), -np.sin(ANGLE_Z)], 0))
    table = np.zeros((3, 4, 2 * MZ, 4, N), BF16)
    for plane in range(4):
        table[0, plane, :, plane] = high
        table[1, plane, :, plane] = high
        table[2, plane, :, plane] = low
    return table.reshape(3 * 128, 4 * N)


def one_hot(hits):
    return jnp.where(hits, 1.0, 0.0).astype(BF16)


def reorder_matrix():
    row = lax.broadcasted_iota(jnp.int32, (C * JL, C * JL), 0)
    column = lax.broadcasted_iota(jnp.int32, (C * JL, C * JL), 1)
    sent, j = row >> 4, row & (JL - 1)
    channel = ((sent >> 4) * 8 + (sent & 7)) * 2 + ((sent >> 3) & 1)
    return one_hot(column == j * C + channel)


def spread_matrix():
    row = lax.broadcasted_iota(jnp.int32, (2 * C, C * C), 0)
    column = lax.broadcasted_iota(jnp.int32, (2 * C, C * C), 1)
    return one_hot((row & (C - 1)) == (column >> 5))


def rows_table():
    return np.repeat(np.eye(C), 8, 0).astype(BF16)


def fold_table():
    table = np.zeros((2, GROUPS, 8, C), BF16)
    for inner in range(2):
        for group in range(GROUPS):
            table[inner, group, :, 2 * group + inner] = 1
    return table.reshape(256, C)


def gelu_slope(h):
    square = h * h
    t = jnp.tanh(h * (TANH_SCALE + (TANH_SCALE * CUBIC) * square))
    inner = h * (0.5 * TANH_SCALE + (1.5 * TANH_SCALE * CUBIC) * square)
    return (0.5 + 0.5 * t) + (1.0 - t * t) * inner


def lane_swap(value, first_sign):
    lanes = lax.broadcasted_iota(jnp.int32, value.shape, value.ndim - 1)
    up = pltpu.roll(value, 128 - MZ, value.ndim - 1)
    down = pltpu.roll(value, MZ, value.ndim - 1)
    return jnp.where((lanes & MZ) == 0, first_sign * up, -first_sign * down)


YB = 32
CHUNKS = N // YB
TILES = YB // 8


def chunk_copy(ref, buffer, sem, chunk):
    rows = pl.ds(YB * chunk, YB)
    copy = pltpu.make_async_copy(ref.at[0, :, :, rows, :], buffer.at[:, :, rows, :], sem)
    copy.start()
    return copy


def whole_copy(ref, buffer, sem):
    copy = pltpu.make_async_copy(ref, buffer, sem)
    copy.start()
    return copy


def spread_lines(value, lhs, tile):
    value = value.reshape(GROUPS, 2, 2, 8, N)
    rows = slice(128 * tile, 128 * tile + 128)
    for inner in range(2):
        for plane in range(2):
            high, low = split(value[:, inner, plane].reshape(GROUPS * 8, N))
            lane = 256 * (2 * inner + plane)
            lhs[rows, lane:lane + 128] = high
            lhs[rows, lane + 128:lane + 256] = low


def transform_z(lhs, ztab_ref, scratch, chunk):
    out = dot(lhs[128 * TILES * chunk:128 * TILES * (chunk + 1), :], ztab_ref[...])
    out = out[:, :128] + out[:, 128:]
    for tile in range(TILES):
        place = YB * chunk + 8 * tile
        scratch[:, place:place + 8, :] = out[128 * tile:128 * tile + 128].reshape(GROUPS, 8, 128)


def transform_y(scratch, ytab_ref, half):
    for pair in range(GROUPS // 2):
        wide = jnp.concatenate([scratch[2 * pair], scratch[2 * pair + 1]], 1)
        high, low = split(wide)
        out = dot(ytab_ref[...], jnp.concatenate([high, low, high], 0))
        for member in range(2):
            mine = out[:, 128 * member:128 * member + 128]
            half[2 * pair + member] = mine[:MY] + lane_swap(mine[MY:], -1.0)


def lay_out(half, send_ref, offset, group_set):
    for jq in range(4):
        block = half[8 * group_set:8 * group_set + 8, JL * jq:JL * jq + JL, :]
        turned = block.reshape(128, 128).T
        for r in range(8):
            row = offset + 8 * group_set + r
            send_ref[pl.ds(jq, MZ, stride=4), row, :] = turned[MZ * r:MZ * r + MZ]


def finish(ytab, lines, half, send, send_hbm, out_sems):
    transform_y(lines, ytab, half)
    copies = []
    for group_set in range(2):
        lay_out(half, send, 0, group_set)
        rows = pl.ds(8 * group_set, 8)
        copies.append(whole_copy(send.at[:, rows], send_hbm.at[:, rows], out_sems.at[group_set]))
    return copies


def line_rows(chunk):
    return pl.ds(128 * TILES * chunk, 128 * TILES)


def gradient_kernel(
    pre_hbm, cot_hbm, ztab_hbm, ytab_hbm, send_hbm, lhs_hbm,
    pre, cot, ztab, ytab, lhs, lines, half, send, sems, tab_sems, out_sems, lhs_sems,
):
    copies = [
        [chunk_copy(ref, buffer, sems.at[chunk, k], chunk) for k, ref, buffer in ((0, pre_hbm, pre), (1, cot_hbm, cot))]
        for chunk in range(CHUNKS)
    ]
    tables = [whole_copy(ztab_hbm, ztab, tab_sems.at[0]), whole_copy(ytab_hbm, ytab, tab_sems.at[1])]
    outs = []
    for chunk in range(CHUNKS):
        for copy in copies[chunk]:
            copy.wait()
        for tile in range(TILES * chunk, TILES * chunk + TILES):
            rows = slice(8 * tile, 8 * tile + 8)
            spread_lines(cot[:, :, rows, :] * gelu_slope(pre[:, :, rows, :]), lhs, tile)
        rows = line_rows(chunk)
        outs.append(whole_copy(lhs.at[rows], lhs_hbm.at[rows], lhs_sems.at[chunk]))
    for table in tables:
        table.wait()
    for chunk in range(CHUNKS):
        transform_z(lhs, ztab, lines, chunk)
    outs += finish(ytab, lines, half, send, send_hbm, out_sems)
    for copy in outs:
        copy.wait()


def in_vmem(count):
    return [pl.BlockSpec(memory_space=pltpu.VMEM) for _ in range(count)]


def vmem_spec():
    return pl.BlockSpec(memory_space=pltpu.VMEM)


def any_spec():
    return pl.BlockSpec(memory_space=pl.ANY)


FIELD = (C, 2, N, N)


PAIR = (N // 8, 256, 256)


def in_hbm(value):
    return pltpu.with_memory_space_constraint(value, pltpu.HBM)


def kept(value):
    return pltpu.with_memory_space_constraint(value, pltpu.VMEM)


LINES = (2048, 1024)


def gradient_spectrum(preact, cotangent):
    ztab, ytab = jnp.asarray(z_tables()), jnp.asarray(y_tables())
    return pl.pallas_call(
        gradient_kernel,
        in_specs=[any_spec()] * 4,
        out_specs=[any_spec()] * 2,
        out_shape=[pltpu.HBM((SPACE, FIRST, 128), F32), pltpu.HBM(LINES, BF16)],
        scratch_shapes=[pltpu.VMEM(FIELD, F32)] * 2 + [
            pltpu.VMEM(ztab.shape, BF16), pltpu.VMEM(ytab.shape, BF16), pltpu.VMEM(LINES, BF16),
            pltpu.VMEM((GROUPS, N, 128), F32), pltpu.VMEM((GROUPS, MY, 128), F32), pltpu.VMEM((SPACE, FIRST, 128), F32),
            pltpu.SemaphoreType.DMA((CHUNKS, 2)), pltpu.SemaphoreType.DMA((2,)), pltpu.SemaphoreType.DMA((2,)),
            pltpu.SemaphoreType.DMA((CHUNKS,)),
        ],
        compiler_params=pltpu.CompilerParams(vmem_limit_bytes=LIMIT),
        name="gradient_spectrum",
    )(in_hbm(preact), in_hbm(cotangent), in_hbm(ztab), in_hbm(ytab))


ACROSS = (((1,), (1,)), ((), ()))


def same_row():
    left = lax.broadcasted_iota(jnp.int32, (256, 256), 0) & 7
    right = lax.broadcasted_iota(jnp.int32, (256, 256), 1) & 7
    return left == right


def tile_parts(lines, tile):
    rows = slice(128 * tile, 128 * tile + 128)
    return [
        jnp.concatenate([
            jnp.concatenate([
                lines[rows, 512 * inner + 256 * plane + part:512 * inner + 256 * plane + part + 128] for plane in range(2)
            ], 1) for inner in range(2)
        ], 0) for part in (0, 128)
    ]


def input_kernel(
    one_ref, lhs_hbm, inp_hbm, ztab_hbm, ytab_hbm, fold_ref, send_hbm,
    g_lines, inp, ztab, ytab, lhs, acc, lines, half, send, sems, tab_sems, out_sems,
):
    always = one_ref[0] >= 0
    copies = []
    for chunk in range(CHUNKS):
        rows = line_rows(chunk)
        copies.append([
            chunk_copy(inp_hbm, inp, sems.at[chunk, 0], chunk),
            whole_copy(lhs_hbm.at[rows], g_lines.at[rows], sems.at[chunk, 1]),
        ])
    tables = [whole_copy(ztab_hbm, ztab, tab_sems.at[0]), whole_copy(ytab_hbm, ytab, tab_sems.at[1])]
    for chunk in range(CHUNKS):
        for copy in copies[chunk]:
            copy.wait()

        @pl.when(always)
        def _():
            for tile in range(TILES * chunk, TILES * chunk + TILES):
                spread_lines(inp[:, :, 8 * tile:8 * tile + 8, :], lhs, tile)

        if chunk == 0:
            tables[0].wait()

        @pl.when(always)
        def _():
            transform_z(lhs, ztab, lines, chunk)

        @pl.when(always)
        def _():
            for tile in range(TILES * chunk, TILES * chunk + TILES):
                g_high, g_low = tile_parts(g_lines, tile)
                i_high, i_low = tile_parts(lhs, tile)
                total = (
                    lax.dot_general(g_high, i_high, ACROSS, preferred_element_type=F32)
                    + lax.dot_general(g_low, i_high, ACROSS, preferred_element_type=F32)
                    + lax.dot_general(g_high, i_low, ACROSS, preferred_element_type=F32)
                )
                if tile == 0:
                    acc[...] = total
                else:
                    acc[...] += total

    diagonal = jnp.where(same_row(), acc[...], 0.0) * NORM
    fold = fold_ref[...].astype(F32)
    folded = jnp.dot(diagonal, fold, preferred_element_type=F32, precision=lax.Precision.HIGHEST)
    summed = lax.dot_general(
        fold, folded, (((0,), (0,)), ((), ())), preferred_element_type=F32,
        precision=lax.Precision.HIGHEST,
    )
    part = jnp.concatenate([summed[8 * q:8 * q + 8, :] for q in range(4)], 1)
    for dest in range(SPACE):
        send[dest, 16:] = part
    rows = pl.ds(16, 8)
    outs = [whole_copy(send.at[:, rows], send_hbm.at[:, rows], out_sems.at[2])]
    tables[1].wait()
    outs += finish(ytab, lines, half, send, send_hbm, out_sems)
    for copy in outs:
        copy.wait()


def input_spectrum(one, lines, inputs):
    ztab, ytab = jnp.asarray(z_tables()), jnp.asarray(y_tables())
    return pl.pallas_call(
        input_kernel,
        in_specs=[pl.BlockSpec(memory_space=pltpu.SMEM)] + [any_spec()] * 4 + [vmem_spec()],
        out_specs=any_spec(),
        out_shape=pltpu.HBM((SPACE, 24, 128), F32),
        scratch_shapes=[
            pltpu.VMEM(LINES, BF16), pltpu.VMEM(FIELD, F32),
            pltpu.VMEM(ztab.shape, BF16), pltpu.VMEM(ytab.shape, BF16), pltpu.VMEM(LINES, BF16),
            pltpu.VMEM((256, 256), F32),
            pltpu.VMEM((GROUPS, N, 128), F32), pltpu.VMEM((GROUPS, MY, 128), F32), pltpu.VMEM((SPACE, 24, 128), F32),
            pltpu.SemaphoreType.DMA((CHUNKS, 2)), pltpu.SemaphoreType.DMA((2,)), pltpu.SemaphoreType.DMA((3,)),
        ],
        compiler_params=pltpu.CompilerParams(vmem_limit_bytes=LIMIT),
        name="input_spectrum",
    )(one, in_hbm(lines), in_hbm(inputs), in_hbm(ztab), in_hbm(ytab), fold_table())


def skip_kernel(lhs_hbm, after_hbm, skip_ref, rows_ref, fold_ref, term_hbm, g_lines, term, sems, out_sems):
    copies = []
    for chunk in range(CHUNKS):
        rows = line_rows(chunk)
        copies.append(whole_copy(lhs_hbm.at[rows], g_lines.at[rows], sems.at[chunk]))
    matrix = []
    for part in split(skip_ref[...]):
        wide = lax.dot_general(rows_ref[...], part, ACROSS, preferred_element_type=F32).astype(BF16)
        wide = lax.dot_general(wide, fold_ref[...], ACROSS, preferred_element_type=F32)
        matrix.append(jnp.where(same_row(), wide, 0.0).astype(BF16))
    matrix = jnp.concatenate(matrix, 0)
    outs = []
    for chunk in range(CHUNKS):
        copies[chunk].wait()
        for tile in range(TILES * chunk, TILES * chunk + TILES):
            rows = slice(8 * tile, 8 * tile + 8)
            g_high, g_low = tile_parts(g_lines, tile)
            out = dot(matrix, g_high)
            out = out[:256] + out[256:] + dot(matrix[:256], g_low)
            for plane in range(2):
                value = out[:, 128 * plane:128 * plane + 128].reshape(C, 8, N)
                term[:, plane, rows, :] = value
        rows = pl.ds(YB * chunk, YB)
        outs.append(whole_copy(term.at[:, :, rows, :], term_hbm.at[:, :, rows, :], out_sems.at[chunk]))
    for copy in outs:
        copy.wait()


def skip_term(lines, after, skip_weight):
    return pl.pallas_call(
        skip_kernel,
        in_specs=[any_spec()] * 2 + in_vmem(3),
        out_specs=any_spec(),
        out_shape=pltpu.HBM(FIELD, F32),
        scratch_shapes=[
            pltpu.VMEM(LINES, BF16), pltpu.VMEM(FIELD, F32),
            pltpu.SemaphoreType.DMA((CHUNKS,)), pltpu.SemaphoreType.DMA((CHUNKS,)),
        ],
        compiler_params=pltpu.CompilerParams(vmem_limit_bytes=LIMIT),
        name="skip_term",
    )(in_hbm(lines), after, skip_weight, rows_table(), fold_table())


FIRST = 16
SECOND = 40


def transform_x(recv_ref, rows_each, offset, xtab_ref, reorder):
    blocks = []
    for q in range(4):
        column = [recv_ref[pl.ds(offset + 4 * q + r, SPACE, stride=rows_each), :] for r in range(4)]
        blocks.append(jnp.concatenate(column, 0))
    high, low = split(jnp.concatenate(blocks, 1))
    out = dot(xtab_ref[...], high)
    spectrum = out[:2 * MX] + out[2 * MX:] + dot(xtab_ref[:2 * MX], low)
    out = dot(jnp.concatenate(split(spectrum), 0), reorder)
    return out[:2 * MX] + out[2 * MX:]


def to_rows(spectrum, scratch):
    for j in range(JL):
        scratch[:, j, :] = spectrum[:, C * j:C * j + C]


WB = 8


def middle_kernel(
    dp_ref, recv_ref, xtab_ref, back_ref, w_hbm, input_hbm, send_hbm, mine_ref, theirs_ref,
    w_ref, spec, wide, dual, send, sems, out_sems,
):
    copies = []
    for block in range(MX // WB):
        rows = pl.ds(WB * block, WB)
        copies.append(whole_copy(w_hbm.at[rows], w_ref.at[rows], sems.at[block]))
    onward = pl.ds(16, 24)
    arriving = whole_copy(input_hbm, send.at[:, onward], out_sems.at[3])
    reorder = reorder_matrix()
    spread = spread_matrix()
    first = dp_ref[0] == 0
    spectrum = transform_x(recv_ref, FIRST, 0, xtab_ref, reorder)
    mine_ref[...] = jnp.where(first, spectrum[:MX], spectrum[MX:])
    theirs_ref[...] = jnp.where(first, spectrum[MX:], spectrum[:MX])
    to_rows(spectrum, spec)

    for block in range(MX // WB):
        start = 32 * (WB * block // 16) + WB * block % 16
        both = jnp.concatenate([spec[start:start + WB], spec[start + 16:start + 16 + WB]], 0)
        high, low = split(both.reshape(2 * WB * JL, C))
        wide[block % 2] = dot(jnp.concatenate([high, low], 1), spread)
        copies[block].wait()
        for local in range(WB):
            total_real, total_imag = None, None
            for tile in range(8):
                lanes = slice(128 * tile, 128 * tile + 128)
                real = wide[block % 2, JL * local:JL * local + JL, lanes]
                imag = wide[block % 2, JL * (WB + local):JL * (WB + local) + JL, lanes]
                m = WB * block + local
                w_real = w_ref[m, :, lanes]
                w_imag = w_ref[m, :, 1024 + 128 * tile:1024 + 128 * tile + 128]
                out_real = w_real * real + w_imag * imag
                out_imag = w_real * imag - w_imag * real
                total_real = out_real if tile == 0 else total_real + out_real
                total_imag = out_imag if tile == 0 else total_imag + out_imag
            for total, place in ((total_real, start + local), (total_imag, start + 16 + local)):
                total = total + pltpu.roll(total, 64, 1)
                dual[place] = total + pltpu.roll(total, 32, 1)

    arriving.wait()
    copies = [whole_copy(send.at[:, onward], send_hbm.at[:, onward], out_sems.at[2])]
    lanes = lax.broadcasted_iota(jnp.int32, (2 * MX, 128), 1) // C
    blocks = []
    for j4 in range(4):
        block = dual[:, 4 * j4, :]
        for k in range(1, 4):
            block = jnp.where(lanes == k, dual[:, 4 * j4 + k, :], block)
        blocks.append(block)
    both = jnp.concatenate(split(jnp.concatenate(blocks, 1)), 0)
    ordered = lax.dot_general(both, reorder, ACROSS, preferred_element_type=F32)
    high, low = split(ordered[:2 * MX] + ordered[2 * MX:])
    out = dot(back_ref[...], jnp.concatenate([high, low, high], 0))
    for half in range(2):
        for q in (2 * half, 2 * half + 1):
            for r in range(4):
                send[:, 4 * q + r, :] = out[SPACE * r:SPACE * r + SPACE, 128 * q:128 * q + 128]
        rows = pl.ds(8 * half, 8)
        copies.append(whole_copy(send.at[:, rows], send_hbm.at[:, rows], sems.at[half]))
    for copy in copies:
        copy.wait()


def middle(dp, received, weights, input_rows):
    return pl.pallas_call(
        middle_kernel,
        in_specs=[pl.BlockSpec(memory_space=pltpu.SMEM)] + in_vmem(3) + [any_spec()] * 2,
        out_specs=[any_spec()] + in_vmem(2),
        out_shape=[
            pltpu.HBM((SPACE, SECOND, 128), F32),
            jax.ShapeDtypeStruct((MX, JL * C), F32),
            jax.ShapeDtypeStruct((MX, JL * C), F32),
        ],
        scratch_shapes=[
            pltpu.VMEM((MX, JL, 2 * C * C), F32), pltpu.VMEM((2 * MX, JL, C), F32),
            pltpu.VMEM((2, 2 * WB * JL, C * C), F32), pltpu.VMEM((2 * MX, JL, 128), F32),
            pltpu.VMEM((SPACE, SECOND, 128), F32),
            pltpu.SemaphoreType.DMA((MX // WB,)), pltpu.SemaphoreType.DMA((4,)),
        ],
        compiler_params=pltpu.CompilerParams(vmem_limit_bytes=LIMIT),
        name="middle",
    )(dp, received, x_tables(), back_x_tables(), in_hbm(weights), in_hbm(input_rows))


def inputs_kernel(dp_ref, recv_ref, theirs_ref, xtab_ref, after_hbm, mine_ref, out_ref):
    spectrum = transform_x(recv_ref, SECOND, 16, xtab_ref, reorder_matrix())
    first = dp_ref[0] == 0
    mine_ref[...] = jnp.where(first, spectrum[:MX], spectrum[MX:])
    out_ref[:MX, :] = theirs_ref[...]
    out_ref[MX:2 * MX, :] = jnp.where(first, spectrum[MX:], spectrum[:MX])
    total = recv_ref[32:40, :]
    for source in range(1, SPACE):
        total = total + recv_ref[SECOND * source + 32:SECOND * source + 40, :]
    out_ref[2 * MX:, :] = jnp.concatenate([total] * 4, 1)


def inputs_spectrum(dp, received, theirs, after):
    return pl.pallas_call(
        inputs_kernel,
        in_specs=[pl.BlockSpec(memory_space=pltpu.SMEM)] + in_vmem(3) + [any_spec()],
        out_specs=in_vmem(2),
        out_shape=[
            jax.ShapeDtypeStruct((MX, JL * C), F32),
            jax.ShapeDtypeStruct((2 * MX + 8, JL * C), F32),
        ],
        compiler_params=pltpu.CompilerParams(vmem_limit_bytes=LIMIT),
        name="inputs_spectrum",
    )(dp, received, theirs, x_tables(), after)


MB = 4


def weight_kernel(
    grad_ref, field_ref, sent_ref, got_ref, out_hbm, skip_ref, grads, fields, wide, out, sems,
):
    spread = spread_matrix()
    to_rows(grad_ref[...], grads.at[0])
    to_rows(got_ref[:MX], grads.at[1])
    for b, value in enumerate((field_ref[...], got_ref[MX:2 * MX])):
        for j in range(JL):
            piece = value[:, C * j:C * j + C]
            fields[b, :, j, :] = jnp.concatenate([piece] * 4, 1)
    copies = []
    for block in range(16 // MB):
        rows = jnp.concatenate(
            [grads[b, 16 * s + MB * block:16 * s + MB * block + MB] for b in range(2) for s in range(2)], 0
        )
        high, low = split(rows.reshape(4 * MB * JL, C))
        wide[...] = dot(jnp.concatenate([high, low], 1), spread)
        for local in range(MB):
            m = MB * block + local
            f = [fields[b, m + 16 * s] for b in range(2) for s in range(2)]
            for tile in range(8):
                lanes = slice(128 * tile, 128 * tile + 128)
                g = [wide[JL * (MB * q + local):JL * (MB * q + local) + JL, lanes] for q in range(4)]
                out[m, :, lanes] = g[0] * f[0] + g[1] * f[1] + g[2] * f[2] + g[3] * f[3]
                out[m, :, 1024 + 128 * tile:1024 + 128 * tile + 128] = (
                    g[1] * f[0] - g[0] * f[1] + g[3] * f[2] - g[2] * f[3]
                )
        rows = pl.ds(MB * block, MB)
        copy = pltpu.make_async_copy(out.at[rows], out_hbm.at[rows], sems.at[block])
        copy.start()
        copies.append(copy)
    total = sent_ref[2 * MX:, :128] + got_ref[2 * MX:, :128]
    for q in range(4):
        skip_ref[8 * q:8 * q + 8, :] = total[:, C * q:C * q + C]
    for copy in copies:
        copy.wait()


def weight_gradient(grad_mine, field_mine, sent, got):
    return pl.pallas_call(
        weight_kernel,
        in_specs=in_vmem(4),
        out_specs=[any_spec(), vmem_spec()],
        out_shape=[pltpu.HBM((16, JL, 2 * C * C), F32), jax.ShapeDtypeStruct((C, C), F32)],
        scratch_shapes=[
            pltpu.VMEM((2, MX, JL, C), F32), pltpu.VMEM((2, MX, JL, 128), F32),
            pltpu.VMEM((4 * MB * JL, C * C), F32), pltpu.VMEM((16, JL, 2 * C * C), F32),
            pltpu.SemaphoreType.DMA((16 // MB,)),
        ],
        compiler_params=pltpu.CompilerParams(vmem_limit_bytes=LIMIT),
        name="weight_gradient",
    )(grad_mine, field_mine, sent, got)


GB = 4


def backward_kernel(
    recv_ref, term_hbm, ytab_ref, ztab_hbm, out_hbm, term, ztab, out, half, lhs, sems, out_sems,
):
    copies = []
    for block in range(GROUPS // GB):
        rows = pl.ds(2 * GB * block, 2 * GB)
        copies.append(whole_copy(term_hbm.at[rows], term.at[rows], sems.at[block]))
        if block == 0:
            ztab_copy = whole_copy(ztab_hbm, ztab, sems.at[GROUPS // GB])
    for jq in range(4):
        for group_set in range(2):
            rows = [recv_ref[pl.ds(jq * SECOND + 8 * group_set + r, MZ, stride=4 * SECOND), :] for r in range(8)]
            turned = jnp.concatenate(rows, 0).T
            half[8 * group_set:8 * group_set + 8, JL * jq:JL * jq + JL, :] = turned.reshape(8, JL, 128)
    outs = []
    for block in range(GROUPS // GB):
        for pair in range(GB // 2):
            both = []
            for member in range(2):
                value = half[GB * block + 2 * pair + member]
                both.append(jnp.concatenate([value, lane_swap(value, -1.0)], 0))
            high, low = split(jnp.concatenate(both, 1))
            lines = dot(ytab_ref[...], jnp.concatenate([high, low, high], 0))
            for member in range(2):
                high, low = split(lines[:, 128 * member:128 * member + 128])
                rows = slice(128 * (2 * pair + member), 128 * (2 * pair + member) + 128)
                lhs[rows, :128] = high
                lhs[rows, 128:256] = low
                lhs[rows, 256:] = high
        if block == 0:
            ztab_copy.wait()
        value = dot(lhs[...], ztab[...])
        copies[block].wait()
        for group in range(GB):
            for inner in range(2):
                for plane in range(2):
                    lane = 128 * (2 * inner + plane)
                    place = 2 * (GB * block + group) + inner
                    out[place, plane] = value[128 * group:128 * group + 128, lane:lane + 128] + term[place, plane]
        rows = pl.ds(2 * GB * block, 2 * GB)
        copy = pltpu.make_async_copy(out.at[rows], out_hbm.at[0, rows], out_sems.at[block])
        copy.start()
        outs.append(copy)
    for copy in outs:
        copy.wait()


def backward(received, term):
    ztab = jnp.asarray(back_z_tables())
    return pl.pallas_call(
        backward_kernel,
        in_specs=[vmem_spec(), any_spec(), vmem_spec(), any_spec()],
        out_specs=any_spec(),
        out_shape=pltpu.HBM((1, C, 2, N, N), F32),
        scratch_shapes=[
            pltpu.VMEM(FIELD, F32), pltpu.VMEM(ztab.shape, BF16), pltpu.VMEM(FIELD, F32),
            pltpu.VMEM((GROUPS, MY, 128), F32), pltpu.VMEM((GB * 128, 384), BF16),
            pltpu.SemaphoreType.DMA((GROUPS // GB + 1,)), pltpu.SemaphoreType.DMA((GROUPS // GB,)),
        ],
        compiler_params=pltpu.CompilerParams(vmem_limit_bytes=LIMIT),
        name="backward",
    )(received, in_hbm(term), back_y_tables(), in_hbm(ztab))


def exchange(sent, rows):
    swapped = lax.all_to_all(sent, "space", 0, 0, tiled=True)
    return swapped.reshape(SPACE * rows, 128)


def body(inputs, preact, cotangent, spectral_weight, skip_weight):
    dp = lax.axis_index("dp").astype(jnp.int32).reshape(1)
    send_grad, lines = gradient_spectrum(preact, cotangent)
    got_grad = exchange(send_grad, FIRST)
    input_rows = input_spectrum(dp, lines, inputs)
    send_dual, grad_mine, grad_theirs = middle(dp, got_grad, spectral_weight, input_rows)
    got_dual = exchange(send_dual, SECOND)
    term = skip_term(lines, grad_mine, skip_weight)
    field_mine, sent = inputs_spectrum(dp, got_dual, grad_theirs, term)
    got = lax.ppermute(sent, "dp", [(0, 1), (1, 0)])
    input_grad = backward(got_dual, term)
    weight_grad, skip_grad = weight_gradient(grad_mine, field_mine, sent, got)
    return input_grad, weight_grad, skip_grad


def solution(mesh):
    in_specs = (
        P("dp", None, "space", None, None),
        P("dp", None, "space", None, None),
        P("dp", None, "space", None, None),
        P(None, "space", None),
        P(),
    )
    out_specs = (P("dp", None, "space", None, None), P("dp", "space", None), P())
    return jax.shard_map(body, mesh=mesh, in_specs=in_specs, out_specs=out_specs, check_vma=False)
```

time: 79.9 us -> 79.1 us (0.990)
  starting transfers between devices: 24.3 us -> 20.7 us
  local copies, waits for them, and re-layouts: 0.04 us -> 2.23 us
  waiting for transfers between devices: 16.1 us -> 17.2 us
    ppermute x2 -> x1, starting transfers between devices: 6.76 us -> 3.61 us  [body(): got = lax.ppermute(sent, 'dp', [(0, 1), (1, 0)])]
    all_to_all x2, waiting for transfers between devices: 14.4 us -> 17.2 us  [exchange(): swapped = lax.all_to_all(sent, 'space', 0, 0, tiled=True)]
    unnamed x12 -> x14, local copies, waits for them, and re-layouts: 0.04 us -> 2.23 us
    ppermute x2 -> x1, waiting for transfers between devices: 1.7 us -> 0.01 us  [body(): got = lax.ppermute(sent, 'dp', [(0, 1), (1, 0)])]
  transfers between devices with their start and end apart: 4 -> 3, of which waited for: 3 -> 2; matrix products, arithmetic and copies ran while one was open for 0% -> 0% of each run, Pallas kernels for 20% -> 25%
where the time goes in v1:
time: 79.1 us; the launch traced here: 78.8 us
  Pallas kernels  37.7 us (48%)
  starting transfers between devices  20.7 us (26%)
  waiting for transfers between devices  17.2 us (22%)
  local copies, waits for them, and re-layouts  2.23 us (3%)
  between operations  0.96 us (1%)
    all_to_all x2, waiting for transfers between devices, exchange(): swapped = lax.all_to_all(sent, 'space', 0, 0, tiled=True)  17.2 us
    all_to_all x2, starting transfers between devices, exchange(): swapped = lax.all_to_all(sent, 'space', 0, 0, tiled=True)  17.1 us
    pallas_call x1, Pallas kernels, input_spectrum(): pl.pallas_call(input_kernel, in_specs=[pl.BlockSpec(memory_space=pltpu.SM...  9.69 us
    pallas_call x1, Pallas kernels, gradient_spectrum(): pl.pallas_call(gradient_kernel, in_specs=[any_spec()] * 4, out_specs=[any...  7.98 us
    pallas_call x1, Pallas kernels, backward(): pl.pallas_call(backward_kernel, in_specs=[vmem_spec(), any_spec(), vmem_s...  5.55 us
    pallas_call x1, Pallas kernels, middle(): pl.pallas_call(middle_kernel, in_specs=[pl.BlockSpec(memory_space=pltpu.S...  5.2 us
    pallas_call x1, Pallas kernels, skip_term(): pl.pallas_call(skip_kernel, in_specs=[any_spec()] * 2 + in_vmem(3), out_s...  4.66 us
    pallas_call x1, Pallas kernels, weight_gradient(): pl.pallas_call(weight_kernel, in_specs=in_vmem(4), out_specs=[any_spec(),...  4.14 us
  transfers between devices with their start and end apart: 3, of which 2 were waited for; matrix products, arithmetic and copies ran while one was open for 0% of the time, Pallas kernels for 25%

profile of v1, /device:TPU:1, one launch (start us, length us, event | category | flops | bytes accessed | tf_op | source)
XLA Modules:
  0.0 78.8 jit_solution(11435272842085427142)
XLA Ops:
  0.6 0.0 copy-start.2
  0.6 8.0 %gradient_spectrum.1 = (f32[64,16,128]{2,1,0:T(8,128)}, bf16[2048,1024]{1,0:T(8,128)(2,1)}) custom-call(f32[1,32,2,128,128]{4,3,2,1,0:T(8,128)} %pre_hbm.1, f32[1,32,2,128,128]{4,3,2,1,0:T(8,128)} %cot_hbm.1, bf16[1024,256]{1,0:T(8,128)(2,1)} %constant.22.clone.ztab_hbm, bf16[128,384]{1,0:T(8,128)(2,1)} %constant.23.clone.ytab_hbm), custom_call_target="tpu_custom_call" | custom-call | tf_op jit(solution)/shard_map/gradient_spectrum/pallas_call | solution.py:280
  8.6 10.3 %all-to-all-start = ((f32[64,16,128]{2,1,0:T(8,128)}), f32[64,16,128]{2,1,0:T(8,128)S(1)}, u32[]{:S(2)}, u32[]{:S(2)}) async-start(f32[64,16,128]{2,1,0:T(8,128)} %get-tuple-element.12), calls=%async_computation | async-start | bytes 1048576 | tf_op jit(solution)/shard_map/all_to_all | solution.py:700
  19.0 0.0 copy-done.2
  19.0 0.0 copy-start.1
  19.0 0.0 copy-start.3
  19.0 9.7 %input_spectrum.1.input_hbm = f32[64,24,128]{2,1,0:T(8,128)} custom-call(s32[1]{0:T(128)} %bitcast.one_ref.dp_ref, bf16[2048,1024]{1,0:T(8,128)(2,1)} %get-tuple-element.13.lhs_hbm, f32[1,32,2,128,128]{4,3,2,1,0:T(8,128)} %inp_hbm.1, bf16[1024,256]{1,0:T(8,128)(2,1)} %constant.22.clone.ztab_hbm, bf16[128,384]{1,0:T(8,128)(2,1)} %constant.23.clone.ytab_hbm, ...), custom_call_target="tpu_custom_call" | custom-call | tf_op jit(solution)/shard_map/input_spectrum/pallas_call | solution.py:380
  28.7 0.0 copy-start.5
  28.7 0.0 copy-start.6
  28.7 2.2 %all-to-all-done = f32[64,16,128]{2,1,0:T(8,128)S(1)} async-done(((f32[64,16,128]{2,1,0:T(8,128)}), f32[64,16,128]{2,1,0:T(8,128)S(1)}, u32[]{:S(2)}, u32[]{:S(2)}) %all-to-all-start) | async-done | bytes 524320 | tf_op jit(solution)/shard_map/all_to_all | solution.py:700
  30.9 0.0 copy-done.1
  30.9 0.0 copy-done.3
  30.9 5.2 %middle.1 = (f32[64,40,128]{2,1,0:T(8,128)}, f32[32,512]{1,0:T(8,128)S(1)}, f32[32,512]{1,0:T(8,128)S(1)}) custom-call(s32[1]{0:T(128)} %bitcast.one_ref.dp_ref, f32[1024,128]{1,0:T(8,128)S(1)} %bitcast.5, bf16[128,256]{1,0:T(8,128)(2,1)S(1)} %copy-done.1, bf16[256,192]{1,0:T(8,128)(2,1)S(1)} %copy-done.3, f32[32,16,2048]{2,1,0:T(8,128)} %w_hbm.1, ...), custom_call_target="tpu_custom_call" | custom-call | tf_op jit(solution)/shard_map/middle/pallas_call | solution.py:529
  36.1 6.7 %all-to-all-start.1 = ((f32[64,40,128]{2,1,0:T(8,128)}), f32[64,40,128]{2,1,0:T(8,128)S(1)}, u32[]{:S(2)}, u32[]{:S(2)}) async-start(f32[64,40,128]{2,1,0:T(8,128)} %get-tuple-element.14), calls=%async_computation.1 | async-start | bytes 2621440 | tf_op jit(solution)/shard_map/all_to_all | solution.py:700
  42.9 0.0 copy-done.5
  42.9 0.0 copy-done.6
  42.9 0.0 copy-start.4
  42.9 4.7 %skip_term.1.term_hbm.after_hbm = f32[32,2,128,128]{3,2,1,0:T(8,128)} custom-call(bf16[2048,1024]{1,0:T(8,128)(2,1)} %get-tuple-element.13.lhs_hbm, f32[32,512]{1,0:T(8,128)S(1)} %get-tuple-element.15.after_hbm.grad_ref, f32[32,32]{1,0:T(8,128)S(1)} %copy-done.6, bf16[256,32]{1,0:T(8,128)(2,1)S(1)} %copy-done.5, bf16[256,32]{1,0:T(8,128)(2,1)S(1)} %copy-done.2), custom_call_target="tpu_custom_call" | custom-call | tf_op jit(solution)/shard_map/skip_term/pallas_call | solution.py:426
  47.6 15.0 %all-to-all-done.1 = f32[64,40,128]{2,1,0:T(8,128)S(1)} async-done(((f32[64,40,128]{2,1,0:T(8,128)}), f32[64,40,128]{2,1,0:T(8,128)S(1)}, u32[]{:S(2)}, u32[]{:S(2)}) %all-to-all-start.1) | async-done | bytes 1310752 | tf_op jit(solution)/shard_map/all_to_all | solution.py:700
  62.6 0.0 copy-start
  62.6 2.2 %copy-done = f32[32,2,128,128]{3,2,1,0:T(8,128)S(1)} copy-done((f32[32,2,128,128]{3,2,1,0:T(8,128)S(1)}, f32[32,2,128,128]{3,2,1,0:T(8,128)}, u32[]{:S(2)}) %copy-start) | copy-done | bytes 4194328
  64.8 0.5 inputs_spectrum.1
  65.3 3.6 %collective-permute-start = (f32[72,512]{1,0:T(8,128)S(1)}, f32[72,512]{1,0:T(8,128)S(1)}, u32[]{:S(2)}, u32[]{:S(2)}) collective-permute-start(f32[72,512]{1,0:T(8,128)S(1)} %get-tuple-element.18.sent_ref), channel_id=1, source_target_pairs={{0,64},{64,0},{1,65},{65,1},{2,66},{66,2},{3,67},{67,3},{4,68},{68... | collective-permute-start | bytes 442376 | tf_op jit(solution)/shard_map/ppermute | solution.py:713
  68.9 0.0 copy-done.4
  68.9 5.6 %backward.1 = f32[1,32,2,128,128]{4,3,2,1,0:T(8,128)} custom-call(f32[2560,128]{1,0:T(8,128)S(1)} %bitcast.4, f32[32,2,128,128]{3,2,1,0:T(8,128)} %skip_term.1.term_hbm.after_hbm, bf16[128,384]{1,0:T(8,128)(2,1)S(1)} %copy-done.4, bf16[384,512]{1,0:T(8,128)(2,1)} %constant.28.clone.ztab_hbm), custom_call_target="tpu_custom_call" | custom-call | tf_op jit(solution)/shard_map/backward/pallas_call | solution.py:684
  74.5 0.0 collective-permute-done.got_ref
  74.5 4.1 %weight_gradient.1 = (f32[16,16,2048]{2,1,0:T(8,128)}, f32[32,32]{1,0:T(8,128)}) custom-call(f32[32,512]{1,0:T(8,128)S(1)} %get-tuple-element.15.after_hbm.grad_ref, f32[32,512]{1,0:T(8,128)S(1)} %get-tuple-element.17.field_ref, f32[72,512]{1,0:T(8,128)S(1)} %get-tuple-element.18.sent_ref, f32[72,512]{1,0:T(8,128)S(1)} %collective-permute-done.got_ref), custom_call_target="tpu_custom_call" | custom-call | tf_op jit(solution)/shard_map/weight_gradient/pallas_call | solution.py:617
Async XLA Ops:
  0.6 18.4 %copy-start.2 = (bf16[256,32]{1,0:T(8,128)(2,1)S(1)}, bf16[256,32]{1,0:T(8,128)(2,1)}, u32[]{:S(2)}) copy-start(bf16[256,32]{1,0:T(8,128)(2,1)} %constant.24.clone.fold_ref) | copy-start | bytes 49156
  8.6 22.3 %all-to-all-start = ((f32[64,16,128]{2,1,0:T(8,128)}), f32[64,16,128]{2,1,0:T(8,128)S(1)}, u32[]{:S(2)}, u32[]{:S(2)}) async-start(f32[64,16,128]{2,1,0:T(8,128)} %get-tuple-element.12), calls=%async_computation | async-start | bytes 1048576 | tf_op jit(solution)/shard_map/all_to_all | solution.py:700
  19.0 11.9 %copy-start.1 = (bf16[128,256]{1,0:T(8,128)(2,1)S(1)}, bf16[128,256]{1,0:T(8,128)(2,1)}, u32[]{:S(2)}) copy-start(bf16[128,256]{1,0:T(8,128)(2,1)} %constant.25.clone.xtab_ref) | copy-start | bytes 196612
  19.0 11.9 %copy-start.3 = (bf16[256,192]{1,0:T(8,128)(2,1)S(1)}, bf16[256,192]{1,0:T(8,128)(2,1)}, u32[]{:S(2)}) copy-start(bf16[256,192]{1,0:T(8,128)(2,1)} %constant.26.clone.back_ref) | copy-start | bytes 294916
  28.7 14.2 %copy-start.5 = (bf16[256,32]{1,0:T(8,128)(2,1)S(1)}, bf16[256,32]{1,0:T(8,128)(2,1)}, u32[]{:S(2)}) copy-start(bf16[256,32]{1,0:T(8,128)(2,1)} %constant.27.clone.rows_ref) | copy-start | bytes 49156
  28.7 14.2 %copy-start.6 = (f32[32,32]{1,0:T(8,128)S(1)}, f32[32,32]{1,0:T(8,128)}, u32[]{:S(2)}) copy-start(f32[32,32]{1,0:T(8,128)} %skip_ref.1) | copy-start | bytes 12292
  36.1 26.4 %all-to-all-start.1 = ((f32[64,40,128]{2,1,0:T(8,128)}), f32[64,40,128]{2,1,0:T(8,128)S(1)}, u32[]{:S(2)}, u32[]{:S(2)}) async-start(f32[64,40,128]{2,1,0:T(8,128)} %get-tuple-element.14), calls=%async_computation.1 | async-start | bytes 2621440 | tf_op jit(solution)/shard_map/all_to_all | solution.py:700
  42.9 26.0 %copy-start.4 = (bf16[128,384]{1,0:T(8,128)(2,1)S(1)}, bf16[128,384]{1,0:T(8,128)(2,1)}, u32[]{:S(2)}) copy-start(bf16[128,384]{1,0:T(8,128)(2,1)} %constant.29.clone.ytab_ref) | copy-start | bytes 294916
  62.6 2.2 %copy-start = (f32[32,2,128,128]{3,2,1,0:T(8,128)S(1)}, f32[32,2,128,128]{3,2,1,0:T(8,128)}, u32[]{:S(2)}) copy-start(f32[32,2,128,128]{3,2,1,0:T(8,128)} %skip_term.1.term_hbm.after_hbm) | copy-start | bytes 12582916
  65.3 9.2 %collective-permute-start = (f32[72,512]{1,0:T(8,128)S(1)}, f32[72,512]{1,0:T(8,128)S(1)}, u32[]{:S(2)}, u32[]{:S(2)}) collective-permute-start(f32[72,512]{1,0:T(8,128)S(1)} %get-tuple-element.18.sent_ref), channel_id=1, source_target_pairs={{0,64},{64,0},{1,65},{65,1},{2,66},{66,2},{3,67},{67,3},{4,68},{68... | collective-permute-start | bytes 442376 | tf_op jit(solution)/shard_map/ppermute | solution.py:713

commit v2 on v1

--- a/solution.py
+++ b/solution.py
@@ -118,8 +118,8 @@
 
 
 def spread_matrix():
-    row = lax.broadcasted_iota(jnp.int32, (2 * C, C * C), 0)
-    column = lax.broadcasted_iota(jnp.int32, (2 * C, C * C), 1)
+    row = lax.broadcasted_iota(jnp.int32, (8 * C, C * C), 0)
+    column = lax.broadcasted_iota(jnp.int32, (8 * C, C * C), 1)
     return one_hot((row & (C - 1)) == (column >> 5))
 
 
@@ -196,22 +196,27 @@
             half[2 * pair + member] = mine[:MY] + lane_swap(mine[MY:], -1.0)
 
 
-def lay_out(half, send_ref, offset, group_set):
+def blocks_of(send):
+    return send.reshape(SPACE, send.shape[0] // SPACE, 128)
+
+
+def lay_out(half, send_ref, group_set):
+    rows_each = send_ref.shape[0] // SPACE
     for jq in range(4):
         block = half[8 * group_set:8 * group_set + 8, JL * jq:JL * jq + JL, :]
         turned = block.reshape(128, 128).T
         for r in range(8):
-            row = offset + 8 * group_set + r
-            send_ref[pl.ds(jq, MZ, stride=4), row, :] = turned[MZ * r:MZ * r + MZ]
+            row = jq * rows_each + 8 * group_set + r
+            send_ref[pl.ds(row, MZ, stride=4 * rows_each), :] = turned[MZ * r:MZ * r + MZ]
 
 
 def finish(ytab, lines, half, send, send_hbm, out_sems):
     transform_y(lines, ytab, half)
     copies = []
     for group_set in range(2):
-        lay_out(half, send, 0, group_set)
+        lay_out(half, send, group_set)
         rows = pl.ds(8 * group_set, 8)
-        copies.append(whole_copy(send.at[:, rows], send_hbm.at[:, rows], out_sems.at[group_set]))
+        copies.append(whole_copy(blocks_of(send).at[:, rows], send_hbm.at[:, rows], out_sems.at[group_set]))
     return copies
 
 
@@ -284,7 +289,7 @@
         out_shape=[pltpu.HBM((SPACE, FIRST, 128), F32), pltpu.HBM(LINES, BF16)],
         scratch_shapes=[pltpu.VMEM(FIELD, F32)] * 2 + [
             pltpu.VMEM(ztab.shape, BF16), pltpu.VMEM(ytab.shape, BF16), pltpu.VMEM(LINES, BF16),
-            pltpu.VMEM((GROUPS, N, 128), F32), pltpu.VMEM((GROUPS, MY, 128), F32), pltpu.VMEM((SPACE, FIRST, 128), F32),
+            pltpu.VMEM((GROUPS, N, 128), F32), pltpu.VMEM((GROUPS, MY, 128), F32), pltpu.VMEM((SPACE * FIRST, 128), F32),
             pltpu.SemaphoreType.DMA((CHUNKS, 2)), pltpu.SemaphoreType.DMA((2,)), pltpu.SemaphoreType.DMA((2,)),
             pltpu.SemaphoreType.DMA((CHUNKS,)),
         ],
@@ -366,9 +371,9 @@
     )
     part = jnp.concatenate([summed[8 * q:8 * q + 8, :] for q in range(4)], 1)
     for dest in range(SPACE):
-        send[dest, 16:] = part
+        send[24 * dest + 16:24 * dest + 24, :] = part
     rows = pl.ds(16, 8)
-    outs = [whole_copy(send.at[:, rows], send_hbm.at[:, rows], out_sems.at[2])]
+    outs = [whole_copy(blocks_of(send).at[:, rows], send_hbm.at[:, rows], out_sems.at[2])]
     tables[1].wait()
     outs += finish(ytab, lines, half, send, send_hbm, out_sems)
     for copy in outs:
@@ -386,7 +391,7 @@
             pltpu.VMEM(LINES, BF16), pltpu.VMEM(FIELD, F32),
             pltpu.VMEM(ztab.shape, BF16), pltpu.VMEM(ytab.shape, BF16), pltpu.VMEM(LINES, BF16),
             pltpu.VMEM((256, 256), F32),
-            pltpu.VMEM((GROUPS, N, 128), F32), pltpu.VMEM((GROUPS, MY, 128), F32), pltpu.VMEM((SPACE, 24, 128), F32),
+            pltpu.VMEM((GROUPS, N, 128), F32), pltpu.VMEM((GROUPS, MY, 128), F32), pltpu.VMEM((SPACE * 24, 128), F32),
             pltpu.SemaphoreType.DMA((CHUNKS, 2)), pltpu.SemaphoreType.DMA((2,)), pltpu.SemaphoreType.DMA((3,)),
         ],
         compiler_params=pltpu.CompilerParams(vmem_limit_bytes=LIMIT),
@@ -454,8 +459,11 @@
 
 
 def to_rows(spectrum, scratch):
+    count = spectrum.shape[0]
+    lanes = lax.broadcasted_iota(jnp.int32, (count, 128), 1) >> 5
     for j in range(JL):
-        scratch[:, j, :] = spectrum[:, C * j:C * j + C]
+        block = spectrum[:, 128 * (j // 4):128 * (j // 4) + 128]
+        scratch[pl.ds(j, count, stride=JL), :] = jnp.where(lanes == j % 4, block, 0.0)
 
 
 WB = 8
@@ -470,7 +478,7 @@
         rows = pl.ds(WB * block, WB)
         copies.append(whole_copy(w_hbm.at[rows], w_ref.at[rows], sems.at[block]))
     onward = pl.ds(16, 24)
-    arriving = whole_copy(input_hbm, send.at[:, onward], out_sems.at[3])
+    arriving = whole_copy(input_hbm, blocks_of(send).at[:, onward], out_sems.at[3])
     reorder = reorder_matrix()
     spread = spread_matrix()
     first = dp_ref[0] == 0
@@ -481,8 +489,8 @@
 
     for block in range(MX // WB):
         start = 32 * (WB * block // 16) + WB * block % 16
-        both = jnp.concatenate([spec[start:start + WB], spec[start + 16:start + 16 + WB]], 0)
-        high, low = split(both.reshape(2 * WB * JL, C))
+        both = jnp.concatenate([spec[JL * k:JL * (k + WB), :] for k in (start, start + 16)], 0)
+        high, low = split(both)
         wide[block % 2] = dot(jnp.concatenate([high, low], 1), spread)
         copies[block].wait()
         for local in range(WB):
@@ -500,16 +508,16 @@
                 total_imag = out_imag if tile == 0 else total_imag + out_imag
             for total, place in ((total_real, start + local), (total_imag, start + 16 + local)):
                 total = total + pltpu.roll(total, 64, 1)
-                dual[place] = total + pltpu.roll(total, 32, 1)
+                dual[JL * place:JL * place + JL, :] = total + pltpu.roll(total, 32, 1)
 
     arriving.wait()
-    copies = [whole_copy(send.at[:, onward], send_hbm.at[:, onward], out_sems.at[2])]
+    copies = [whole_copy(blocks_of(send).at[:, onward], send_hbm.at[:, onward], out_sems.at[2])]
     lanes = lax.broadcasted_iota(jnp.int32, (2 * MX, 128), 1) // C
     blocks = []
     for j4 in range(4):
-        block = dual[:, 4 * j4, :]
+        block = dual[pl.ds(4 * j4, 2 * MX, stride=JL), :]
         for k in range(1, 4):
-            block = jnp.where(lanes == k, dual[:, 4 * j4 + k, :], block)
+            block = jnp.where(lanes == k, dual[pl.ds(4 * j4 + k, 2 * MX, stride=JL), :], block)
         blocks.append(block)
     both = jnp.concatenate(split(jnp.concatenate(blocks, 1)), 0)
     ordered = lax.dot_general(both, reorder, ACROSS, preferred_element_type=F32)
@@ -518,9 +526,9 @@
     for half in range(2):
         for q in (2 * half, 2 * half + 1):
             for r in range(4):
-                send[:, 4 * q + r, :] = out[SPACE * r:SPACE * r + SPACE, 128 * q:128 * q + 128]
+                send[pl.ds(4 * q + r, SPACE, stride=SECOND), :] = out[SPACE * r:SPACE * r + SPACE, 128 * q:128 * q + 128]
         rows = pl.ds(8 * half, 8)
-        copies.append(whole_copy(send.at[:, rows], send_hbm.at[:, rows], sems.at[half]))
+        copies.append(whole_copy(blocks_of(send).at[:, rows], send_hbm.at[:, rows], sems.at[half]))
     for copy in copies:
         copy.wait()
 
@@ -536,9 +544,9 @@
             jax.ShapeDtypeStruct((MX, JL * C), F32),
         ],
         scratch_shapes=[
-            pltpu.VMEM((MX, JL, 2 * C * C), F32), pltpu.VMEM((2 * MX, JL, C), F32),
-            pltpu.VMEM((2, 2 * WB * JL, C * C), F32), pltpu.VMEM((2 * MX, JL, 128), F32),
-            pltpu.VMEM((SPACE, SECOND, 128), F32),
+            pltpu.VMEM((MX, JL, 2 * C * C), F32), pltpu.VMEM((2 * MX * JL, 128), F32),
+            pltpu.VMEM((2, 2 * WB * JL, C * C), F32), pltpu.VMEM((2 * MX * JL, 128), F32),
+            pltpu.VMEM((SPACE * SECOND, 128), F32),
             pltpu.SemaphoreType.DMA((MX // WB,)), pltpu.SemaphoreType.DMA((4,)),
         ],
         compiler_params=pltpu.CompilerParams(vmem_limit_bytes=LIMIT),
@@ -569,7 +577,7 @@
         ],
         compiler_params=pltpu.CompilerParams(vmem_limit_bytes=LIMIT),
         name="inputs_spectrum",
-    )(dp, received, theirs, x_tables(), after)
+    )(dp, received, theirs, x_tables(), in_hbm(after))
 
 
 MB = 4
@@ -584,17 +592,17 @@
     for b, value in enumerate((field_ref[...], got_ref[MX:2 * MX])):
         for j in range(JL):
             piece = value[:, C * j:C * j + C]
-            fields[b, :, j, :] = jnp.concatenate([piece] * 4, 1)
+            fields[b, pl.ds(j, MX, stride=JL), :] = jnp.concatenate([piece] * 4, 1)
     copies = []
     for block in range(16 // MB):
         rows = jnp.concatenate(
-            [grads[b, 16 * s + MB * block:16 * s + MB * block + MB] for b in range(2) for s in range(2)], 0
+            [grads[b, JL * k:JL * (k + MB), :] for b in range(2) for k in (MB * block, 16 + MB * block)], 0
         )
-        high, low = split(rows.reshape(4 * MB * JL, C))
+        high, low = split(rows)
         wide[...] = dot(jnp.concatenate([high, low], 1), spread)
         for local in range(MB):
             m = MB * block + local
-            f = [fields[b, m + 16 * s] for b in range(2) for s in range(2)]
+            f = [fields[b, JL * k:JL * k + JL, :] for b in range(2) for k in (m, m + 16)]
             for tile in range(8):
                 lanes = slice(128 * tile, 128 * tile + 128)
                 g = [wide[JL * (MB * q + local):JL * (MB * q + local) + JL, lanes] for q in range(4)]
@@ -620,7 +628,7 @@
         out_specs=[any_spec(), vmem_spec()],
         out_shape=[pltpu.HBM((16, JL, 2 * C * C), F32), jax.ShapeDtypeStruct((C, C), F32)],
         scratch_shapes=[
-            pltpu.VMEM((2, MX, JL, C), F32), pltpu.VMEM((2, MX, JL, 128), F32),
+            pltpu.VMEM((2, MX * JL, 128), F32), pltpu.VMEM((2, MX * JL, 128), F32),
             pltpu.VMEM((4 * MB * JL, C * C), F32), pltpu.VMEM((16, JL, 2 * C * C), F32),
             pltpu.SemaphoreType.DMA((16 // MB,)),
         ],

time: 79.1 us -> 75 us (0.948)
  local copies, waits for them, and re-layouts: 2.23 us -> 0.04 us
  Pallas kernels: 37.7 us -> 36.1 us
    unnamed x14 -> x12, local copies, waits for them, and re-layouts: 2.23 us -> 0.04 us
    pallas_call x1, Pallas kernels: 4.14 us -> 2.73 us  [weight_gradient(): pl.pallas_call(weight_kernel, in_specs=in_vmem(4), out_specs=[any_spec(),...]
  transfers between devices with their start and end apart: 3 -> 3, of which waited for: 2 -> 2; matrix products, arithmetic and copies ran while one was open for 0% -> 0% of each run, Pallas kernels for 25% -> 27%
where the time goes in v2:
time: 75 us; the launch traced here: 74.7 us
  Pallas kernels  36.1 us (48%)
  starting transfers between devices  20.5 us (27%)
  waiting for transfers between devices  17.2 us (23%)
  between operations  0.94 us (1%)
    all_to_all x2, waiting for transfers between devices, exchange(): swapped = lax.all_to_all(sent, 'space', 0, 0, tiled=True)  17.2 us
    all_to_all x2, starting transfers between devices, exchange(): swapped = lax.all_to_all(sent, 'space', 0, 0, tiled=True)  17.1 us
    pallas_call x1, Pallas kernels, input_spectrum(): pl.pallas_call(input_kernel, in_specs=[pl.BlockSpec(memory_space=pltpu.SM...  9.7 us
    pallas_call x1, Pallas kernels, gradient_spectrum(): pl.pallas_call(gradient_kernel, in_specs=[any_spec()] * 4, out_specs=[any...  8.01 us
    pallas_call x1, Pallas kernels, backward(): pl.pallas_call(backward_kernel, in_specs=[vmem_spec(), any_spec(), vmem_s...  5.55 us
    pallas_call x1, Pallas kernels, middle(): pl.pallas_call(middle_kernel, in_specs=[pl.BlockSpec(memory_space=pltpu.S...  4.93 us
    pallas_call x1, Pallas kernels, skip_term(): pl.pallas_call(skip_kernel, in_specs=[any_spec()] * 2 + in_vmem(3), out_s...  4.63 us
    ppermute x1, starting transfers between devices, body(): got = lax.ppermute(sent, 'dp', [(0, 1), (1, 0)])  3.38 us
  transfers between devices with their start and end apart: 3, of which 2 were waited for; matrix products, arithmetic and copies ran while one was open for 0% of the time, Pallas kernels for 27%

profile of v2, /device:TPU:1, one launch (start us, length us, event | category | flops | bytes accessed | tf_op | source)
XLA Modules:
  0.0 74.7 jit_solution(15839745404221902192)
XLA Ops:
  0.6 0.0 copy-start.1
  0.6 8.0 %gradient_spectrum.1 = (f32[64,16,128]{2,1,0:T(8,128)}, bf16[2048,1024]{1,0:T(8,128)(2,1)}) custom-call(f32[1,32,2,128,128]{4,3,2,1,0:T(8,128)} %pre_hbm.1, f32[1,32,2,128,128]{4,3,2,1,0:T(8,128)} %cot_hbm.1, bf16[1024,256]{1,0:T(8,128)(2,1)} %constant.22.clone.ztab_hbm, bf16[128,384]{1,0:T(8,128)(2,1)} %constant.23.clone.ytab_hbm), custom_call_target="tpu_custom_call" | custom-call | tf_op jit(solution)/shard_map/gradient_spectrum/pallas_call | solution.py:285
  8.7 10.4 %all-to-all-start = ((f32[64,16,128]{2,1,0:T(8,128)}), f32[64,16,128]{2,1,0:T(8,128)S(1)}, u32[]{:S(2)}, u32[]{:S(2)}) async-start(f32[64,16,128]{2,1,0:T(8,128)} %get-tuple-element.12), calls=%async_computation | async-start | bytes 1048576 | tf_op jit(solution)/shard_map/all_to_all | solution.py:708
  19.0 0.0 copy-done.1
  19.0 0.0 copy-start
  19.0 0.0 copy-start.2
  19.1 9.7 %input_spectrum.1.input_hbm = f32[64,24,128]{2,1,0:T(8,128)} custom-call(s32[1]{0:T(128)} %bitcast.one_ref.dp_ref, bf16[2048,1024]{1,0:T(8,128)(2,1)} %get-tuple-element.13.lhs_hbm, f32[1,32,2,128,128]{4,3,2,1,0:T(8,128)} %inp_hbm.1, bf16[1024,256]{1,0:T(8,128)(2,1)} %constant.22.clone.ztab_hbm, bf16[128,384]{1,0:T(8,128)(2,1)} %constant.23.clone.ytab_hbm, ...), custom_call_target="tpu_custom_call" | custom-call | tf_op jit(solution)/shard_map/input_spectrum/pallas_call | solution.py:385
  28.8 0.0 copy-start.4
  28.8 0.0 copy-start.5
  28.8 2.2 %all-to-all-done = f32[64,16,128]{2,1,0:T(8,128)S(1)} async-done(((f32[64,16,128]{2,1,0:T(8,128)}), f32[64,16,128]{2,1,0:T(8,128)S(1)}, u32[]{:S(2)}, u32[]{:S(2)}) %all-to-all-start) | async-done | bytes 524320 | tf_op jit(solution)/shard_map/all_to_all | solution.py:708
  31.0 0.0 copy-done
  31.0 0.0 copy-done.2
  31.0 4.9 %middle.1 = (f32[64,40,128]{2,1,0:T(8,128)}, f32[32,512]{1,0:T(8,128)S(1)}, f32[32,512]{1,0:T(8,128)S(1)}) custom-call(s32[1]{0:T(128)} %bitcast.one_ref.dp_ref, f32[1024,128]{1,0:T(8,128)S(1)} %bitcast.5, bf16[128,256]{1,0:T(8,128)(2,1)S(1)} %copy-done, bf16[256,192]{1,0:T(8,128)(2,1)S(1)} %copy-done.2, f32[32,16,2048]{2,1,0:T(8,128)} %w_hbm.1, ...), custom_call_target="tpu_custom_call" | custom-call | tf_op jit(solution)/shard_map/middle/pallas_call | solution.py:537
  35.9 6.8 %all-to-all-start.1 = ((f32[64,40,128]{2,1,0:T(8,128)}), f32[64,40,128]{2,1,0:T(8,128)S(1)}, u32[]{:S(2)}, u32[]{:S(2)}) async-start(f32[64,40,128]{2,1,0:T(8,128)} %get-tuple-element.14), calls=%async_computation.1 | async-start | bytes 2621440 | tf_op jit(solution)/shard_map/all_to_all | solution.py:708
  42.7 0.0 copy-done.4
  42.7 0.0 copy-done.5
  42.7 4.6 %skip_term.1.term_hbm.after_hbm = f32[32,2,128,128]{3,2,1,0:T(8,128)} custom-call(bf16[2048,1024]{1,0:T(8,128)(2,1)} %get-tuple-element.13.lhs_hbm, f32[32,512]{1,0:T(8,128)S(1)} %get-tuple-element.15.after_hbm.grad_ref, f32[32,32]{1,0:T(8,128)S(1)} %copy-done.5, bf16[256,32]{1,0:T(8,128)(2,1)S(1)} %copy-done.4, bf16[256,32]{1,0:T(8,128)(2,1)S(1)} %copy-done.1), custom_call_target="tpu_custom_call" | custom-call | tf_op jit(solution)/shard_map/skip_term/pallas_call | solution.py:431
  47.3 0.0 copy-start.3
  47.4 15.0 %all-to-all-done.1 = f32[64,40,128]{2,1,0:T(8,128)S(1)} async-done(((f32[64,40,128]{2,1,0:T(8,128)}), f32[64,40,128]{2,1,0:T(8,128)S(1)}, u32[]{:S(2)}, u32[]{:S(2)}) %all-to-all-start.1) | async-done | bytes 1310752 | tf_op jit(solution)/shard_map/all_to_all | solution.py:708
  62.4 0.5 inputs_spectrum.1
  62.9 3.4 %collective-permute-start = (f32[72,512]{1,0:T(8,128)S(1)}, f32[72,512]{1,0:T(8,128)S(1)}, u32[]{:S(2)}, u32[]{:S(2)}) collective-permute-start(f32[72,512]{1,0:T(8,128)S(1)} %get-tuple-element.18.sent_ref), channel_id=1, source_target_pairs={{0,64},{64,0},{1,65},{65,1},{2,66},{66,2},{3,67},{67,3},{4,68},{68... | collective-permute-start | bytes 442376 | tf_op jit(solution)/shard_map/ppermute | solution.py:721
  66.3 0.0 copy-done.3
  66.3 5.6 %backward.1 = f32[1,32,2,128,128]{4,3,2,1,0:T(8,128)} custom-call(f32[2560,128]{1,0:T(8,128)S(1)} %bitcast.4, f32[32,2,128,128]{3,2,1,0:T(8,128)} %skip_term.1.term_hbm.after_hbm, bf16[128,384]{1,0:T(8,128)(2,1)S(1)} %copy-done.3, bf16[384,512]{1,0:T(8,128)(2,1)} %constant.28.clone.ztab_hbm), custom_call_target="tpu_custom_call" | custom-call | tf_op jit(solution)/shard_map/backward/pallas_call | solution.py:692
  71.8 0.0 collective-permute-done.got_ref
  71.8 2.7 %weight_gradient.1 = (f32[16,16,2048]{2,1,0:T(8,128)}, f32[32,32]{1,0:T(8,128)}) custom-call(f32[32,512]{1,0:T(8,128)S(1)} %get-tuple-element.15.after_hbm.grad_ref, f32[32,512]{1,0:T(8,128)S(1)} %get-tuple-element.17.field_ref, f32[72,512]{1,0:T(8,128)S(1)} %get-tuple-element.18.sent_ref, f32[72,512]{1,0:T(8,128)S(1)} %collective-permute-done.got_ref), custom_call_target="tpu_custom_call" | custom-call | tf_op jit(solution)/shard_map/weight_gradient/pallas_call | solution.py:625
Async XLA Ops:
  0.6 18.4 %copy-start.1 = (bf16[256,32]{1,0:T(8,128)(2,1)S(1)}, bf16[256,32]{1,0:T(8,128)(2,1)}, u32[]{:S(2)}) copy-start(bf16[256,32]{1,0:T(8,128)(2,1)} %constant.24.clone.fold_ref) | copy-start | bytes 49156
  8.7 22.3 %all-to-all-start = ((f32[64,16,128]{2,1,0:T(8,128)}), f32[64,16,128]{2,1,0:T(8,128)S(1)}, u32[]{:S(2)}, u32[]{:S(2)}) async-start(f32[64,16,128]{2,1,0:T(8,128)} %get-tuple-element.12), calls=%async_computation | async-start | bytes 1048576 | tf_op jit(solution)/shard_map/all_to_all | solution.py:708
  19.0 11.9 %copy-start = (bf16[128,256]{1,0:T(8,128)(2,1)S(1)}, bf16[128,256]{1,0:T(8,128)(2,1)}, u32[]{:S(2)}) copy-start(bf16[128,256]{1,0:T(8,128)(2,1)} %constant.25.clone.xtab_ref) | copy-start | bytes 196612
  19.0 11.9 %copy-start.2 = (bf16[256,192]{1,0:T(8,128)(2,1)S(1)}, bf16[256,192]{1,0:T(8,128)(2,1)}, u32[]{:S(2)}) copy-start(bf16[256,192]{1,0:T(8,128)(2,1)} %constant.26.clone.back_ref) | copy-start | bytes 294916
  28.8 13.9 %copy-start.4 = (bf16[256,32]{1,0:T(8,128)(2,1)S(1)}, bf16[256,32]{1,0:T(8,128)(2,1)}, u32[]{:S(2)}) copy-start(bf16[256,32]{1,0:T(8,128)(2,1)} %constant.27.clone.rows_ref) | copy-start | bytes 49156
  28.8 13.9 %copy-start.5 = (f32[32,32]{1,0:T(8,128)S(1)}, f32[32,32]{1,0:T(8,128)}, u32[]{:S(2)}) copy-start(f32[32,32]{1,0:T(8,128)} %skip_ref.1) | copy-start | bytes 12292
  35.9 26.5 %all-to-all-start.1 = ((f32[64,40,128]{2,1,0:T(8,128)}), f32[64,40,128]{2,1,0:T(8,128)S(1)}, u32[]{:S(2)}, u32[]{:S(2)}) async-start(f32[64,40,128]{2,1,0:T(8,128)} %get-tuple-element.14), calls=%async_computation.1 | async-start | bytes 2621440 | tf_op jit(solution)/shard_map/all_to_all | solution.py:708
  47.3 18.9 %copy-start.3 = (bf16[128,384]{1,0:T(8,128)(2,1)S(1)}, bf16[128,384]{1,0:T(8,128)(2,1)}, u32[]{:S(2)}) copy-start(bf16[128,384]{1,0:T(8,128)(2,1)} %constant.29.clone.ytab_ref) | copy-start | bytes 294916
  62.9 8.9 %collective-permute-start = (f32[72,512]{1,0:T(8,128)S(1)}, f32[72,512]{1,0:T(8,128)S(1)}, u32[]{:S(2)}, u32[]{:S(2)}) collective-permute-start(f32[72,512]{1,0:T(8,128)S(1)} %get-tuple-element.18.sent_ref), channel_id=1, source_target_pairs={{0,64},{64,0},{1,65},{65,1},{2,66},{66,2},{3,67},{67,3},{4,68},{68... | collective-permute-start | bytes 442376 | tf_op jit(solution)/shard_map/ppermute | solution.py:721

commit v3 on v2

--- a/solution.py
+++ b/solution.py
@@ -186,8 +186,8 @@
         scratch[:, place:place + 8, :] = out[128 * tile:128 * tile + 128].reshape(GROUPS, 8, 128)
 
 
-def transform_y(scratch, ytab_ref, half):
-    for pair in range(GROUPS // 2):
+def transform_y(scratch, ytab_ref, half, group_set):
+    for pair in range(4 * group_set, 4 * group_set + 4):
         wide = jnp.concatenate([scratch[2 * pair], scratch[2 * pair + 1]], 1)
         high, low = split(wide)
         out = dot(ytab_ref[...], jnp.concatenate([high, low, high], 0))
@@ -211,8 +211,9 @@
 
 
 def finish(ytab, lines, half, send, send_hbm, out_sems):
-    transform_y(lines, ytab, half)
     copies = []
+    transform_y(lines, ytab, half, 0)
+    transform_y(lines, ytab, half, 1)
     for group_set in range(2):
         lay_out(half, send, group_set)
         rows = pl.ds(8 * group_set, 8)
@@ -240,6 +241,7 @@
         for tile in range(TILES * chunk, TILES * chunk + TILES):
             rows = slice(8 * tile, 8 * tile + 8)
             spread_lines(cot[:, :, rows, :] * gelu_slope(pre[:, :, rows, :]), lhs, tile)
+    for chunk in range(CHUNKS):
         rows = line_rows(chunk)
         outs.append(whole_copy(lhs.at[rows], lhs_hbm.at[rows], lhs_sems.at[chunk]))
     for table in tables:
@@ -319,7 +321,7 @@
 
 
 def input_kernel(
-    one_ref, lhs_hbm, inp_hbm, ztab_hbm, ytab_hbm, fold_ref, send_hbm,
+    one_ref, lhs_hbm, inp_hbm, ztab_hbm, ytab_hbm, w_hbm, fold_ref, send_hbm, w_ref,
     g_lines, inp, ztab, ytab, lhs, acc, lines, half, send, sems, tab_sems, out_sems,
 ):
     always = one_ref[0] >= 0
@@ -331,6 +333,7 @@
             whole_copy(lhs_hbm.at[rows], g_lines.at[rows], sems.at[chunk, 1]),
         ])
     tables = [whole_copy(ztab_hbm, ztab, tab_sems.at[0]), whole_copy(ytab_hbm, ytab, tab_sems.at[1])]
+    ahead = whole_copy(w_hbm.at[pl.ds(0, WB)], w_ref, tab_sems.at[2])
     for chunk in range(CHUNKS):
         for copy in copies[chunk]:
             copy.wait()
@@ -376,27 +379,28 @@
     outs = [whole_copy(blocks_of(send).at[:, rows], send_hbm.at[:, rows], out_sems.at[2])]
     tables[1].wait()
     outs += finish(ytab, lines, half, send, send_hbm, out_sems)
+    ahead.wait()
     for copy in outs:
         copy.wait()
 
 
-def input_spectrum(one, lines, inputs):
+def input_spectrum(one, lines, inputs, weights):
     ztab, ytab = jnp.asarray(z_tables()), jnp.asarray(y_tables())
     return pl.pallas_call(
         input_kernel,
-        in_specs=[pl.BlockSpec(memory_space=pltpu.SMEM)] + [any_spec()] * 4 + [vmem_spec()],
-        out_specs=any_spec(),
-        out_shape=pltpu.HBM((SPACE, 24, 128), F32),
+        in_specs=[pl.BlockSpec(memory_space=pltpu.SMEM)] + [any_spec()] * 5 + [vmem_spec()],
+        out_specs=[any_spec(), vmem_spec()],
+        out_shape=[pltpu.HBM((SPACE, 24, 128), F32), pltpu.VMEM((WB, JL, 2 * C * C), F32)],
         scratch_shapes=[
             pltpu.VMEM(LINES, BF16), pltpu.VMEM(FIELD, F32),
             pltpu.VMEM(ztab.shape, BF16), pltpu.VMEM(ytab.shape, BF16), pltpu.VMEM(LINES, BF16),
             pltpu.VMEM((256, 256), F32),
             pltpu.VMEM((GROUPS, N, 128), F32), pltpu.VMEM((GROUPS, MY, 128), F32), pltpu.VMEM((SPACE * 24, 128), F32),
-            pltpu.SemaphoreType.DMA((CHUNKS, 2)), pltpu.SemaphoreType.DMA((2,)), pltpu.SemaphoreType.DMA((3,)),
+            pltpu.SemaphoreType.DMA((CHUNKS, 2)), pltpu.SemaphoreType.DMA((3,)), pltpu.SemaphoreType.DMA((3,)),
         ],
         compiler_params=pltpu.CompilerParams(vmem_limit_bytes=LIMIT),
         name="input_spectrum",
-    )(one, in_hbm(lines), in_hbm(inputs), in_hbm(ztab), in_hbm(ytab), fold_table())
+    )(one, in_hbm(lines), in_hbm(inputs), in_hbm(ztab), in_hbm(ytab), in_hbm(weights), fold_table())
 
 
 def skip_kernel(lhs_hbm, after_hbm, skip_ref, rows_ref, fold_ref, term_hbm, g_lines, term, sems, out_sems):
@@ -470,11 +474,11 @@
 
 
 def middle_kernel(
-    dp_ref, recv_ref, xtab_ref, back_ref, w_hbm, input_hbm, send_hbm, mine_ref, theirs_ref,
+    dp_ref, recv_ref, xtab_ref, back_ref, early_ref, w_hbm, input_hbm, send_hbm, mine_ref, theirs_ref,
     w_ref, spec, wide, dual, send, sems, out_sems,
 ):
-    copies = []
-    for block in range(MX // WB):
+    copies = [None]
+    for block in range(1, MX // WB):
         rows = pl.ds(WB * block, WB)
         copies.append(whole_copy(w_hbm.at[rows], w_ref.at[rows], sems.at[block]))
     onward = pl.ds(16, 24)
@@ -492,7 +496,8 @@
         both = jnp.concatenate([spec[JL * k:JL * (k + WB), :] for k in (start, start + 16)], 0)
         high, low = split(both)
         wide[block % 2] = dot(jnp.concatenate([high, low], 1), spread)
-        copies[block].wait()
+        if block > 0:
+            copies[block].wait()
         for local in range(WB):
             total_real, total_imag = None, None
             for tile in range(8):
@@ -500,8 +505,9 @@
                 real = wide[block % 2, JL * local:JL * local + JL, lanes]
                 imag = wide[block % 2, JL * (WB + local):JL * (WB + local) + JL, lanes]
                 m = WB * block + local
-                w_real = w_ref[m, :, lanes]
-                w_imag = w_ref[m, :, 1024 + 128 * tile:1024 + 128 * tile + 128]
+                w_real = early_ref[m, :, lanes] if block == 0 else w_ref[m, :, lanes]
+                far = slice(1024 + 128 * tile, 1024 + 128 * tile + 128)
+                w_imag = early_ref[m, :, far] if block == 0 else w_ref[m, :, far]
                 out_real = w_real * real + w_imag * imag
                 out_imag = w_real * imag - w_imag * real
                 total_real = out_real if tile == 0 else total_real + out_real
@@ -522,21 +528,24 @@
     both = jnp.concatenate(split(jnp.concatenate(blocks, 1)), 0)
     ordered = lax.dot_general(both, reorder, ACROSS, preferred_element_type=F32)
     high, low = split(ordered[:2 * MX] + ordered[2 * MX:])
-    out = dot(back_ref[...], jnp.concatenate([high, low, high], 0))
+    wide_lines = jnp.concatenate([high, low, high], 0)
     for half in range(2):
-        for q in (2 * half, 2 * half + 1):
+        out = dot(back_ref[...], wide_lines[:, 256 * half:256 * half + 256])
+        for k in range(2):
             for r in range(4):
-                send[pl.ds(4 * q + r, SPACE, stride=SECOND), :] = out[SPACE * r:SPACE * r + SPACE, 128 * q:128 * q + 128]
+                send[pl.ds(4 * (2 * half + k) + r, SPACE, stride=SECOND), :] = (
+                    out[SPACE * r:SPACE * r + SPACE, 128 * k:128 * k + 128]
+                )
         rows = pl.ds(8 * half, 8)
-        copies.append(whole_copy(blocks_of(send).at[:, rows], send_hbm.at[:, rows], sems.at[half]))
+        copies.append(whole_copy(blocks_of(send).at[:, rows], send_hbm.at[:, rows], out_sems.at[half]))
     for copy in copies:
         copy.wait()
 
 
-def middle(dp, received, weights, input_rows):
+def middle(dp, received, early, weights, input_rows):
     return pl.pallas_call(
         middle_kernel,
-        in_specs=[pl.BlockSpec(memory_space=pltpu.SMEM)] + in_vmem(3) + [any_spec()] * 2,
+        in_specs=[pl.BlockSpec(memory_space=pltpu.SMEM)] + in_vmem(4) + [any_spec()] * 2,
         out_specs=[any_spec()] + in_vmem(2),
         out_shape=[
             pltpu.HBM((SPACE, SECOND, 128), F32),
@@ -551,7 +560,7 @@
         ],
         compiler_params=pltpu.CompilerParams(vmem_limit_bytes=LIMIT),
         name="middle",
-    )(dp, received, x_tables(), back_x_tables(), in_hbm(weights), in_hbm(input_rows))
+    )(dp, received, x_tables(), back_x_tables(), kept(early), in_hbm(weights), in_hbm(input_rows))
 
 
 def inputs_kernel(dp_ref, recv_ref, theirs_ref, xtab_ref, after_hbm, mine_ref, out_ref):
@@ -671,8 +680,8 @@
                 lhs[rows, 256:] = high
         if block == 0:
             ztab_copy.wait()
-        value = dot(lhs[...], ztab[...])
         copies[block].wait()
+        value = jnp.concatenate([dot(lhs[256 * k:256 * k + 256, :], ztab[...]) for k in range(GB // 2)], 0)
         for group in range(GB):
             for inner in range(2):
                 for plane in range(2):
@@ -713,8 +722,8 @@
     dp = lax.axis_index("dp").astype(jnp.int32).reshape(1)
     send_grad, lines = gradient_spectrum(preact, cotangent)
     got_grad = exchange(send_grad, FIRST)
-    input_rows = input_spectrum(dp, lines, inputs)
-    send_dual, grad_mine, grad_theirs = middle(dp, got_grad, spectral_weight, input_rows)
+    input_rows, early = input_spectrum(dp, lines, inputs, spectral_weight)
+    send_dual, grad_mine, grad_theirs = middle(dp, got_grad, early, spectral_weight, input_rows)
     got_dual = exchange(send_dual, SECOND)
     term = skip_term(lines, grad_mine, skip_weight)
     field_mine, sent = inputs_spectrum(dp, got_dual, grad_theirs, term)

time: 75 us -> 72.3 us (0.964)
  Pallas kernels: 36.1 us -> 33.3 us
    pallas_call x1, Pallas kernels: 5.55 us -> 4.52 us  [backward(): pl.pallas_call(backward_kernel, in_specs=[vmem_spec(), any_spec(), vmem_s...]
  transfers between devices with their start and end apart: 3 -> 3, of which waited for: 2 -> 2; matrix products, arithmetic and copies ran while one was open for 0% -> 0% of each run, Pallas kernels for 27% -> 26%
where the time goes in v3:
time: 72.3 us; the launch traced here: 72 us
  Pallas kernels  33.3 us (46%)
  starting transfers between devices  20.2 us (28%)
  waiting for transfers between devices  17.5 us (24%)
  between operations  0.93 us (1%)
    all_to_all x2, waiting for transfers between devices, exchange(): swapped = lax.all_to_all(sent, 'space', 0, 0, tiled=True)  17.5 us
    all_to_all x2, starting transfers between devices, exchange(): swapped = lax.all_to_all(sent, 'space', 0, 0, tiled=True)  16.9 us
    pallas_call x1, Pallas kernels, input_spectrum(): pl.pallas_call(input_kernel, in_specs=[pl.BlockSpec(memory_space=pltpu.SM...  9.45 us
    pallas_call x1, Pallas kernels, gradient_spectrum(): pl.pallas_call(gradient_kernel, in_specs=[any_spec()] * 4, out_specs=[any...  7.3 us
    pallas_call x1, Pallas kernels, skip_term(): pl.pallas_call(skip_kernel, in_specs=[any_spec()] * 2 + in_vmem(3), out_s...  4.62 us
    pallas_call x1, Pallas kernels, backward(): pl.pallas_call(backward_kernel, in_specs=[vmem_spec(), any_spec(), vmem_s...  4.52 us
    pallas_call x1, Pallas kernels, middle(): pl.pallas_call(middle_kernel, in_specs=[pl.BlockSpec(memory_space=pltpu.S...  4.2 us
    ppermute x1, starting transfers between devices, body(): got = lax.ppermute(sent, 'dp', [(0, 1), (1, 0)])  3.37 us
  transfers between devices with their start and end apart: 3, of which 2 were waited for; matrix products, arithmetic and copies ran while one was open for 0% of the time, Pallas kernels for 26%

profile of v3, /device:TPU:1, one launch (start us, length us, event | category | flops | bytes accessed | tf_op | source)
XLA Modules:
  0.0 72.0 jit_solution(17262999539063520562)
XLA Ops:
  0.6 0.0 copy-start.1
  0.6 7.3 %gradient_spectrum.1 = (f32[64,16,128]{2,1,0:T(8,128)}, bf16[2048,1024]{1,0:T(8,128)(2,1)}) custom-call(f32[1,32,2,128,128]{4,3,2,1,0:T(8,128)} %pre_hbm.1, f32[1,32,2,128,128]{4,3,2,1,0:T(8,128)} %cot_hbm.1, bf16[1024,256]{1,0:T(8,128)(2,1)} %constant.22.clone.ztab_hbm, bf16[128,384]{1,0:T(8,128)(2,1)} %constant.23.clone.ytab_hbm), custom_call_target="tpu_custom_call" | custom-call | tf_op jit(solution)/shard_map/gradient_spectrum/pallas_call | solution.py:287
  7.9 10.4 %all-to-all-start = ((f32[64,16,128]{2,1,0:T(8,128)}), f32[64,16,128]{2,1,0:T(8,128)S(1)}, u32[]{:S(2)}, u32[]{:S(2)}) async-start(f32[64,16,128]{2,1,0:T(8,128)} %get-tuple-element.14), calls=%async_computation | async-start | bytes 1048576 | tf_op jit(solution)/shard_map/all_to_all | solution.py:717
  18.3 0.0 copy-done.1
  18.3 0.0 copy-start
  18.3 0.0 copy-start.2
  18.4 9.5 %input_spectrum.1 = (f32[64,24,128]{2,1,0:T(8,128)}, f32[8,16,2048]{2,1,0:T(8,128)S(1)}) custom-call(s32[1]{0:T(128)} %bitcast.one_ref.dp_ref, bf16[2048,1024]{1,0:T(8,128)(2,1)} %get-tuple-element.15.lhs_hbm, f32[1,32,2,128,128]{4,3,2,1,0:T(8,128)} %inp_hbm.1, bf16[1024,256]{1,0:T(8,128)(2,1)} %constant.22.clone.ztab_hbm, ...), custom_call_target="tpu_custom_call" | custom-call | tf_op jit(solution)/shard_map/input_spectrum/pallas_call | solution.py:389
  27.8 2.5 %all-to-all-done = f32[64,16,128]{2,1,0:T(8,128)S(1)} async-done(((f32[64,16,128]{2,1,0:T(8,128)}), f32[64,16,128]{2,1,0:T(8,128)S(1)}, u32[]{:S(2)}, u32[]{:S(2)}) %all-to-all-start) | async-done | bytes 524320 | tf_op jit(solution)/shard_map/all_to_all | solution.py:717
  30.3 0.0 copy-done
  30.3 0.0 copy-done.2
  30.3 0.0 copy-start.4
  30.3 0.0 copy-start.5
  30.3 4.2 %middle.1 = (f32[64,40,128]{2,1,0:T(8,128)}, f32[32,512]{1,0:T(8,128)S(1)}, f32[32,512]{1,0:T(8,128)S(1)}) custom-call(s32[1]{0:T(128)} %bitcast.one_ref.dp_ref, f32[1024,128]{1,0:T(8,128)S(1)} %bitcast.5, bf16[128,256]{1,0:T(8,128)(2,1)S(1)} %copy-done, bf16[256,192]{1,0:T(8,128)(2,1)S(1)} %copy-done.2, f32[8,16,2048]{2,1,0:T(8,128)S(1)} %get-tuple-element.16.early_ref, ...), custom_call_target="tpu_custom_call" | custom-call | tf_op jit(solution)/shard_map/middle/pallas_call | solution.py:546
  34.5 6.5 %all-to-all-start.1 = ((f32[64,40,128]{2,1,0:T(8,128)}), f32[64,40,128]{2,1,0:T(8,128)S(1)}, u32[]{:S(2)}, u32[]{:S(2)}) async-start(f32[64,40,128]{2,1,0:T(8,128)} %get-tuple-element.18), calls=%async_computation.1 | async-start | bytes 2621440 | tf_op jit(solution)/shard_map/all_to_all | solution.py:717
  41.0 0.0 copy-done.4
  41.0 0.0 copy-done.5
  41.0 4.6 %skip_term.1.term_hbm.after_hbm = f32[32,2,128,128]{3,2,1,0:T(8,128)} custom-call(bf16[2048,1024]{1,0:T(8,128)(2,1)} %get-tuple-element.15.lhs_hbm, f32[32,512]{1,0:T(8,128)S(1)} %get-tuple-element.19.after_hbm.grad_ref, f32[32,32]{1,0:T(8,128)S(1)} %copy-done.5, bf16[256,32]{1,0:T(8,128)(2,1)S(1)} %copy-done.4, bf16[256,32]{1,0:T(8,128)(2,1)S(1)} %copy-done.1), custom_call_target="tpu_custom_call" | custom-call | tf_op jit(solution)/shard_map/skip_term/pallas_call | solution.py:435
  45.6 0.0 copy-start.3
  45.7 15.0 %all-to-all-done.1 = f32[64,40,128]{2,1,0:T(8,128)S(1)} async-done(((f32[64,40,128]{2,1,0:T(8,128)}), f32[64,40,128]{2,1,0:T(8,128)S(1)}, u32[]{:S(2)}, u32[]{:S(2)}) %all-to-all-start.1) | async-done | bytes 1310752 | tf_op jit(solution)/shard_map/all_to_all | solution.py:717
  60.7 0.5 inputs_spectrum.1
  61.2 3.4 %collective-permute-start = (f32[72,512]{1,0:T(8,128)S(1)}, f32[72,512]{1,0:T(8,128)S(1)}, u32[]{:S(2)}, u32[]{:S(2)}) collective-permute-start(f32[72,512]{1,0:T(8,128)S(1)} %get-tuple-element.22.sent_ref), channel_id=1, source_target_pairs={{0,64},{64,0},{1,65},{65,1},{2,66},{66,2},{3,67},{67,3},{4,68},{68... | collective-permute-start | bytes 442376 | tf_op jit(solution)/shard_map/ppermute | solution.py:730
  64.6 0.0 copy-done.3
  64.6 4.5 %backward.1 = f32[1,32,2,128,128]{4,3,2,1,0:T(8,128)} custom-call(f32[2560,128]{1,0:T(8,128)S(1)} %bitcast.4, f32[32,2,128,128]{3,2,1,0:T(8,128)} %skip_term.1.term_hbm.after_hbm, bf16[128,384]{1,0:T(8,128)(2,1)S(1)} %copy-done.3, bf16[384,512]{1,0:T(8,128)(2,1)} %constant.28.clone.ztab_hbm), custom_call_target="tpu_custom_call" | custom-call | tf_op jit(solution)/shard_map/backward/pallas_call | solution.py:701
  69.1 0.0 collective-permute-done.got_ref
  69.1 2.7 %weight_gradient.1 = (f32[16,16,2048]{2,1,0:T(8,128)}, f32[32,32]{1,0:T(8,128)}) custom-call(f32[32,512]{1,0:T(8,128)S(1)} %get-tuple-element.19.after_hbm.grad_ref, f32[32,512]{1,0:T(8,128)S(1)} %get-tuple-element.21.field_ref, f32[72,512]{1,0:T(8,128)S(1)} %get-tuple-element.22.sent_ref, f32[72,512]{1,0:T(8,128)S(1)} %collective-permute-done.got_ref), custom_call_target="tpu_custom_call" | custom-call | tf_op jit(solution)/shard_map/weight_gradient/pallas_call | solution.py:634
Async XLA Ops:
  0.6 17.7 %copy-start.1 = (bf16[256,32]{1,0:T(8,128)(2,1)S(1)}, bf16[256,32]{1,0:T(8,128)(2,1)}, u32[]{:S(2)}) copy-start(bf16[256,32]{1,0:T(8,128)(2,1)} %constant.24.clone.fold_ref) | copy-start | bytes 49156
  7.9 22.3 %all-to-all-start = ((f32[64,16,128]{2,1,0:T(8,128)}), f32[64,16,128]{2,1,0:T(8,128)S(1)}, u32[]{:S(2)}, u32[]{:S(2)}) async-start(f32[64,16,128]{2,1,0:T(8,128)} %get-tuple-element.14), calls=%async_computation | async-start | bytes 1048576 | tf_op jit(solution)/shard_map/all_to_all | solution.py:717
  18.3 11.9 %copy-start = (bf16[128,256]{1,0:T(8,128)(2,1)S(1)}, bf16[128,256]{1,0:T(8,128)(2,1)}, u32[]{:S(2)}) copy-start(bf16[128,256]{1,0:T(8,128)(2,1)} %constant.25.clone.xtab_ref) | copy-start | bytes 196612
  18.3 11.9 %copy-start.2 = (bf16[256,192]{1,0:T(8,128)(2,1)S(1)}, bf16[256,192]{1,0:T(8,128)(2,1)}, u32[]{:S(2)}) copy-start(bf16[256,192]{1,0:T(8,128)(2,1)} %constant.26.clone.back_ref) | copy-start | bytes 294916
  30.3 10.7 %copy-start.4 = (bf16[256,32]{1,0:T(8,128)(2,1)S(1)}, bf16[256,32]{1,0:T(8,128)(2,1)}, u32[]{:S(2)}) copy-start(bf16[256,32]{1,0:T(8,128)(2,1)} %constant.27.clone.rows_ref) | copy-start | bytes 49156
  30.3 10.7 %copy-start.5 = (f32[32,32]{1,0:T(8,128)S(1)}, f32[32,32]{1,0:T(8,128)}, u32[]{:S(2)}) copy-start(f32[32,32]{1,0:T(8,128)} %skip_ref.1) | copy-start | bytes 12292
  34.5 26.2 %all-to-all-start.1 = ((f32[64,40,128]{2,1,0:T(8,128)}), f32[64,40,128]{2,1,0:T(8,128)S(1)}, u32[]{:S(2)}, u32[]{:S(2)}) async-start(f32[64,40,128]{2,1,0:T(8,128)} %get-tuple-element.18), calls=%async_computation.1 | async-start | bytes 2621440 | tf_op jit(solution)/shard_map/all_to_all | solution.py:717
  45.6 18.9 %copy-start.3 = (bf16[128,384]{1,0:T(8,128)(2,1)S(1)}, bf16[128,384]{1,0:T(8,128)(2,1)}, u32[]{:S(2)}) copy-start(bf16[128,384]{1,0:T(8,128)(2,1)} %constant.29.clone.ytab_ref) | copy-start | bytes 294916
  61.2 7.9 %collective-permute-start = (f32[72,512]{1,0:T(8,128)S(1)}, f32[72,512]{1,0:T(8,128)S(1)}, u32[]{:S(2)}, u32[]{:S(2)}) collective-permute-start(f32[72,512]{1,0:T(8,128)S(1)} %get-tuple-element.22.sent_ref), channel_id=1, source_target_pairs={{0,64},{64,0},{1,65},{65,1},{2,66},{66,2},{3,67},{67,3},{4,68},{68... | collective-permute-start | bytes 442376 | tf_op jit(solution)/shard_map/ppermute | solution.py:730

commit v4 on v3

--- a/solution.py
+++ b/solution.py
@@ -333,7 +333,7 @@
             whole_copy(lhs_hbm.at[rows], g_lines.at[rows], sems.at[chunk, 1]),
         ])
     tables = [whole_copy(ztab_hbm, ztab, tab_sems.at[0]), whole_copy(ytab_hbm, ytab, tab_sems.at[1])]
-    ahead = whole_copy(w_hbm.at[pl.ds(0, WB)], w_ref, tab_sems.at[2])
+    ahead = whole_copy(w_hbm.at[pl.ds(0, EARLY * WB)], w_ref, tab_sems.at[2])
     for chunk in range(CHUNKS):
         for copy in copies[chunk]:
             copy.wait()
@@ -390,7 +390,7 @@
         input_kernel,
         in_specs=[pl.BlockSpec(memory_space=pltpu.SMEM)] + [any_spec()] * 5 + [vmem_spec()],
         out_specs=[any_spec(), vmem_spec()],
-        out_shape=[pltpu.HBM((SPACE, 24, 128), F32), pltpu.VMEM((WB, JL, 2 * C * C), F32)],
+        out_shape=[pltpu.HBM((SPACE, 24, 128), F32), pltpu.VMEM((EARLY * WB, JL, 2 * C * C), F32)],
         scratch_shapes=[
             pltpu.VMEM(LINES, BF16), pltpu.VMEM(FIELD, F32),
             pltpu.VMEM(ztab.shape, BF16), pltpu.VMEM(ytab.shape, BF16), pltpu.VMEM(LINES, BF16),
@@ -471,14 +471,15 @@
 
 
 WB = 8
+EARLY = 2
 
 
 def middle_kernel(
     dp_ref, recv_ref, xtab_ref, back_ref, early_ref, w_hbm, input_hbm, send_hbm, mine_ref, theirs_ref,
     w_ref, spec, wide, dual, send, sems, out_sems,
 ):
-    copies = [None]
-    for block in range(1, MX // WB):
+    copies = [None] * EARLY
+    for block in range(EARLY, MX // WB):
         rows = pl.ds(WB * block, WB)
         copies.append(whole_copy(w_hbm.at[rows], w_ref.at[rows], sems.at[block]))
     onward = pl.ds(16, 24)
@@ -496,7 +497,7 @@
         both = jnp.concatenate([spec[JL * k:JL * (k + WB), :] for k in (start, start + 16)], 0)
         high, low = split(both)
         wide[block % 2] = dot(jnp.concatenate([high, low], 1), spread)
-        if block > 0:
+        if block >= EARLY:
             copies[block].wait()
         for local in range(WB):
             total_real, total_imag = None, None
@@ -505,9 +506,9 @@
                 real = wide[block % 2, JL * local:JL * local + JL, lanes]
                 imag = wide[block % 2, JL * (WB + local):JL * (WB + local) + JL, lanes]
                 m = WB * block + local
-                w_real = early_ref[m, :, lanes] if block == 0 else w_ref[m, :, lanes]
+                w_real = early_ref[m, :, lanes] if block < EARLY else w_ref[m, :, lanes]
                 far = slice(1024 + 128 * tile, 1024 + 128 * tile + 128)
-                w_imag = early_ref[m, :, far] if block == 0 else w_ref[m, :, far]
+                w_imag = early_ref[m, :, far] if block < EARLY else w_ref[m, :, far]
                 out_real = w_real * real + w_imag * imag
                 out_imag = w_real * imag - w_imag * real
                 total_real = out_real if tile == 0 else total_real + out_real

time: 72.3 us -> 71.8 us (level)
  no operation moved by 1% of the time
where the time goes in v4:
time: 71.8 us; the launch traced here: 71.5 us
  Pallas kernels  32.8 us (46%)
  starting transfers between devices  20.2 us (28%)
  waiting for transfers between devices  17.5 us (24%)
  between operations  0.93 us (1%)
    all_to_all x2, waiting for transfers between devices, exchange(): swapped = lax.all_to_all(sent, 'space', 0, 0, tiled=True)  17.5 us
    all_to_all x2, starting transfers between devices, exchange(): swapped = lax.all_to_all(sent, 'space', 0, 0, tiled=True)  16.9 us
    pallas_call x1, Pallas kernels, input_spectrum(): pl.pallas_call(input_kernel, in_specs=[pl.BlockSpec(memory_space=pltpu.SM...  9.45 us
    pallas_call x1, Pallas kernels, gradient_spectrum(): pl.pallas_call(gradient_kernel, in_specs=[any_spec()] * 4, out_specs=[any...  7.3 us
    pallas_call x1, Pallas kernels, skip_term(): pl.pallas_call(skip_kernel, in_specs=[any_spec()] * 2 + in_vmem(3), out_s...  4.62 us
    pallas_call x1, Pallas kernels, backward(): pl.pallas_call(backward_kernel, in_specs=[vmem_spec(), any_spec(), vmem_s...  4.52 us
    pallas_call x1, Pallas kernels, middle(): pl.pallas_call(middle_kernel, in_specs=[pl.BlockSpec(memory_space=pltpu.S...  3.72 us
    ppermute x1, starting transfers between devices, body(): got = lax.ppermute(sent, 'dp', [(0, 1), (1, 0)])  3.37 us
  transfers between devices with their start and end apart: 3, of which 2 were waited for; matrix products, arithmetic and copies ran while one was open for 0% of the time, Pallas kernels for 26%

profile of v4, /device:TPU:1, one launch (start us, length us, event | category | flops | bytes accessed | tf_op | source)
XLA Modules:
  0.0 71.5 jit_solution(3867000629934280836)
XLA Ops:
  0.6 0.0 copy-start.1
  0.6 7.3 %gradient_spectrum.1 = (f32[64,16,128]{2,1,0:T(8,128)}, bf16[2048,1024]{1,0:T(8,128)(2,1)}) custom-call(f32[1,32,2,128,128]{4,3,2,1,0:T(8,128)} %pre_hbm.1, f32[1,32,2,128,128]{4,3,2,1,0:T(8,128)} %cot_hbm.1, bf16[1024,256]{1,0:T(8,128)(2,1)} %constant.22.clone.ztab_hbm, bf16[128,384]{1,0:T(8,128)(2,1)} %constant.23.clone.ytab_hbm), custom_call_target="tpu_custom_call" | custom-call | tf_op jit(solution)/shard_map/gradient_spectrum/pallas_call | solution.py:287
  7.9 10.4 %all-to-all-start = ((f32[64,16,128]{2,1,0:T(8,128)}), f32[64,16,128]{2,1,0:T(8,128)S(1)}, u32[]{:S(2)}, u32[]{:S(2)}) async-start(f32[64,16,128]{2,1,0:T(8,128)} %get-tuple-element.14), calls=%async_computation | async-start | bytes 1048576 | tf_op jit(solution)/shard_map/all_to_all | solution.py:718
  18.3 0.0 copy-done.1
  18.3 0.0 copy-start
  18.3 0.0 copy-start.2
  18.4 9.5 %input_spectrum.1 = (f32[64,24,128]{2,1,0:T(8,128)}, f32[16,16,2048]{2,1,0:T(8,128)S(1)}) custom-call(s32[1]{0:T(128)} %bitcast.one_ref.dp_ref, bf16[2048,1024]{1,0:T(8,128)(2,1)} %get-tuple-element.15.lhs_hbm, f32[1,32,2,128,128]{4,3,2,1,0:T(8,128)} %inp_hbm.1, bf16[1024,256]{1,0:T(8,128)(2,1)} %constant.22.clone.ztab_hbm, ...), custom_call_target="tpu_custom_call" | custom-call | tf_op jit(solution)/shard_map/input_spectrum/pallas_call | solution.py:389
  27.8 2.5 %all-to-all-done = f32[64,16,128]{2,1,0:T(8,128)S(1)} async-done(((f32[64,16,128]{2,1,0:T(8,128)}), f32[64,16,128]{2,1,0:T(8,128)S(1)}, u32[]{:S(2)}, u32[]{:S(2)}) %all-to-all-start) | async-done | bytes 524320 | tf_op jit(solution)/shard_map/all_to_all | solution.py:718
  30.3 0.0 copy-done
  30.3 0.0 copy-done.2
  30.3 0.0 copy-start.4
  30.3 0.0 copy-start.5
  30.3 3.7 %middle.1 = (f32[64,40,128]{2,1,0:T(8,128)}, f32[32,512]{1,0:T(8,128)S(1)}, f32[32,512]{1,0:T(8,128)S(1)}) custom-call(s32[1]{0:T(128)} %bitcast.one_ref.dp_ref, f32[1024,128]{1,0:T(8,128)S(1)} %bitcast.5, bf16[128,256]{1,0:T(8,128)(2,1)S(1)} %copy-done, bf16[256,192]{1,0:T(8,128)(2,1)S(1)} %copy-done.2, f32[16,16,2048]{2,1,0:T(8,128)S(1)} %get-tuple-element.16.early_ref, ...), custom_call_target="tpu_custom_call" | custom-call | tf_op jit(solution)/shard_map/middle/pallas_call | solution.py:547
  34.0 6.5 %all-to-all-start.1 = ((f32[64,40,128]{2,1,0:T(8,128)}), f32[64,40,128]{2,1,0:T(8,128)S(1)}, u32[]{:S(2)}, u32[]{:S(2)}) async-start(f32[64,40,128]{2,1,0:T(8,128)} %get-tuple-element.18), calls=%async_computation.1 | async-start | bytes 2621440 | tf_op jit(solution)/shard_map/all_to_all | solution.py:718
  40.5 0.0 copy-done.4
  40.5 0.0 copy-done.5
  40.5 4.6 %skip_term.1.term_hbm.after_hbm = f32[32,2,128,128]{3,2,1,0:T(8,128)} custom-call(bf16[2048,1024]{1,0:T(8,128)(2,1)} %get-tuple-element.15.lhs_hbm, f32[32,512]{1,0:T(8,128)S(1)} %get-tuple-element.19.after_hbm.grad_ref, f32[32,32]{1,0:T(8,128)S(1)} %copy-done.5, bf16[256,32]{1,0:T(8,128)(2,1)S(1)} %copy-done.4, bf16[256,32]{1,0:T(8,128)(2,1)S(1)} %copy-done.1), custom_call_target="tpu_custom_call" | custom-call | tf_op jit(solution)/shard_map/skip_term/pallas_call | solution.py:435
  45.2 0.0 copy-start.3
  45.2 15.0 %all-to-all-done.1 = f32[64,40,128]{2,1,0:T(8,128)S(1)} async-done(((f32[64,40,128]{2,1,0:T(8,128)}), f32[64,40,128]{2,1,0:T(8,128)S(1)}, u32[]{:S(2)}, u32[]{:S(2)}) %all-to-all-start.1) | async-done | bytes 1310752 | tf_op jit(solution)/shard_map/all_to_all | solution.py:718
  60.2 0.5 inputs_spectrum.1
  60.7 3.4 %collective-permute-start = (f32[72,512]{1,0:T(8,128)S(1)}, f32[72,512]{1,0:T(8,128)S(1)}, u32[]{:S(2)}, u32[]{:S(2)}) collective-permute-start(f32[72,512]{1,0:T(8,128)S(1)} %get-tuple-element.22.sent_ref), channel_id=1, source_target_pairs={{0,64},{64,0},{1,65},{65,1},{2,66},{66,2},{3,67},{67,3},{4,68},{68... | collective-permute-start | bytes 442376 | tf_op jit(solution)/shard_map/ppermute | solution.py:731
  64.1 0.0 copy-done.3
  64.1 4.5 %backward.1 = f32[1,32,2,128,128]{4,3,2,1,0:T(8,128)} custom-call(f32[2560,128]{1,0:T(8,128)S(1)} %bitcast.4, f32[32,2,128,128]{3,2,1,0:T(8,128)} %skip_term.1.term_hbm.after_hbm, bf16[128,384]{1,0:T(8,128)(2,1)S(1)} %copy-done.3, bf16[384,512]{1,0:T(8,128)(2,1)} %constant.28.clone.ztab_hbm), custom_call_target="tpu_custom_call" | custom-call | tf_op jit(solution)/shard_map/backward/pallas_call | solution.py:702
  68.6 0.0 collective-permute-done.got_ref
  68.6 2.7 %weight_gradient.1 = (f32[16,16,2048]{2,1,0:T(8,128)}, f32[32,32]{1,0:T(8,128)}) custom-call(f32[32,512]{1,0:T(8,128)S(1)} %get-tuple-element.19.after_hbm.grad_ref, f32[32,512]{1,0:T(8,128)S(1)} %get-tuple-element.21.field_ref, f32[72,512]{1,0:T(8,128)S(1)} %get-tuple-element.22.sent_ref, f32[72,512]{1,0:T(8,128)S(1)} %collective-permute-done.got_ref), custom_call_target="tpu_custom_call" | custom-call | tf_op jit(solution)/shard_map/weight_gradient/pallas_call | solution.py:635
Async XLA Ops:
  0.6 17.7 %copy-start.1 = (bf16[256,32]{1,0:T(8,128)(2,1)S(1)}, bf16[256,32]{1,0:T(8,128)(2,1)}, u32[]{:S(2)}) copy-start(bf16[256,32]{1,0:T(8,128)(2,1)} %constant.24.clone.fold_ref) | copy-start | bytes 49156
  7.9 22.3 %all-to-all-start = ((f32[64,16,128]{2,1,0:T(8,128)}), f32[64,16,128]{2,1,0:T(8,128)S(1)}, u32[]{:S(2)}, u32[]{:S(2)}) async-start(f32[64,16,128]{2,1,0:T(8,128)} %get-tuple-element.14), calls=%async_computation | async-start | bytes 1048576 | tf_op jit(solution)/shard_map/all_to_all | solution.py:718
  18.3 11.9 %copy-start = (bf16[128,256]{1,0:T(8,128)(2,1)S(1)}, bf16[128,256]{1,0:T(8,128)(2,1)}, u32[]{:S(2)}) copy-start(bf16[128,256]{1,0:T(8,128)(2,1)} %constant.25.clone.xtab_ref) | copy-start | bytes 196612
  18.3 11.9 %copy-start.2 = (bf16[256,192]{1,0:T(8,128)(2,1)S(1)}, bf16[256,192]{1,0:T(8,128)(2,1)}, u32[]{:S(2)}) copy-start(bf16[256,192]{1,0:T(8,128)(2,1)} %constant.26.clone.back_ref) | copy-start | bytes 294916
  30.3 10.3 %copy-start.4 = (bf16[256,32]{1,0:T(8,128)(2,1)S(1)}, bf16[256,32]{1,0:T(8,128)(2,1)}, u32[]{:S(2)}) copy-start(bf16[256,32]{1,0:T(8,128)(2,1)} %constant.27.clone.rows_ref) | copy-start | bytes 49156
  30.3 10.3 %copy-start.5 = (f32[32,32]{1,0:T(8,128)S(1)}, f32[32,32]{1,0:T(8,128)}, u32[]{:S(2)}) copy-start(f32[32,32]{1,0:T(8,128)} %skip_ref.1) | copy-start | bytes 12292
  34.0 26.2 %all-to-all-start.1 = ((f32[64,40,128]{2,1,0:T(8,128)}), f32[64,40,128]{2,1,0:T(8,128)S(1)}, u32[]{:S(2)}, u32[]{:S(2)}) async-start(f32[64,40,128]{2,1,0:T(8,128)} %get-tuple-element.18), calls=%async_computation.1 | async-start | bytes 2621440 | tf_op jit(solution)/shard_map/all_to_all | solution.py:718
  45.2 18.9 %copy-start.3 = (bf16[128,384]{1,0:T(8,128)(2,1)S(1)}, bf16[128,384]{1,0:T(8,128)(2,1)}, u32[]{:S(2)}) copy-start(bf16[128,384]{1,0:T(8,128)(2,1)} %constant.29.clone.ytab_ref) | copy-start | bytes 294916
  60.7 7.9 %collective-permute-start = (f32[72,512]{1,0:T(8,128)S(1)}, f32[72,512]{1,0:T(8,128)S(1)}, u32[]{:S(2)}, u32[]{:S(2)}) collective-permute-start(f32[72,512]{1,0:T(8,128)S(1)} %get-tuple-element.22.sent_ref), channel_id=1, source_target_pairs={{0,64},{64,0},{1,65},{65,1},{2,66},{66,2},{3,67},{67,3},{4,68},{68... | collective-permute-start | bytes 442376 | tf_op jit(solution)/shard_map/ppermute | solution.py:731

commit v5 on v4

--- a/solution.py
+++ b/solution.py
@@ -154,8 +154,8 @@
 TILES = YB // 8
 
 
-def chunk_copy(ref, buffer, sem, chunk):
-    rows = pl.ds(YB * chunk, YB)
+def chunk_copy(ref, buffer, sem, chunk, size=YB):
+    rows = pl.ds(size * chunk, size)
     copy = pltpu.make_async_copy(ref.at[0, :, :, rows, :], buffer.at[:, :, rows, :], sem)
     copy.start()
     return copy
@@ -230,15 +230,15 @@
     pre, cot, ztab, ytab, lhs, lines, half, send, sems, tab_sems, out_sems, lhs_sems,
 ):
     copies = [
-        [chunk_copy(ref, buffer, sems.at[chunk, k], chunk) for k, ref, buffer in ((0, pre_hbm, pre), (1, cot_hbm, cot))]
-        for chunk in range(CHUNKS)
+        [chunk_copy(ref, buffer, sems.at[chunk, k], chunk, 16) for k, ref, buffer in ((0, pre_hbm, pre), (1, cot_hbm, cot))]
+        for chunk in range(N // 16)
     ]
     tables = [whole_copy(ztab_hbm, ztab, tab_sems.at[0]), whole_copy(ytab_hbm, ytab, tab_sems.at[1])]
     outs = []
-    for chunk in range(CHUNKS):
+    for chunk in range(N // 16):
         for copy in copies[chunk]:
             copy.wait()
-        for tile in range(TILES * chunk, TILES * chunk + TILES):
+        for tile in (2 * chunk, 2 * chunk + 1):
             rows = slice(8 * tile, 8 * tile + 8)
             spread_lines(cot[:, :, rows, :] * gelu_slope(pre[:, :, rows, :]), lhs, tile)
     for chunk in range(CHUNKS):
@@ -292,7 +292,7 @@
         scratch_shapes=[pltpu.VMEM(FIELD, F32)] * 2 + [
             pltpu.VMEM(ztab.shape, BF16), pltpu.VMEM(ytab.shape, BF16), pltpu.VMEM(LINES, BF16),
             pltpu.VMEM((GROUPS, N, 128), F32), pltpu.VMEM((GROUPS, MY, 128), F32), pltpu.VMEM((SPACE * FIRST, 128), F32),
-            pltpu.SemaphoreType.DMA((CHUNKS, 2)), pltpu.SemaphoreType.DMA((2,)), pltpu.SemaphoreType.DMA((2,)),
+            pltpu.SemaphoreType.DMA((N // 16, 2)), pltpu.SemaphoreType.DMA((2,)), pltpu.SemaphoreType.DMA((2,)),
             pltpu.SemaphoreType.DMA((CHUNKS,)),
         ],
         compiler_params=pltpu.CompilerParams(vmem_limit_bytes=LIMIT),
@@ -590,7 +590,7 @@
     )(dp, received, theirs, x_tables(), in_hbm(after))
 
 
-MB = 4
+MB = 2
 
 
 def weight_kernel(

time: 71.8 us -> 71.5 us (level)
  no operation moved by 1% of the time
where the time goes in v5:
time: 71.5 us; the launch traced here: 71.3 us
  Pallas kernels  32.6 us (46%)
  starting transfers between devices  20.2 us (28%)
  waiting for transfers between devices  17.5 us (24%)
  between operations  0.93 us (1%)
    all_to_all x2, waiting for transfers between devices, exchange(): swapped = lax.all_to_all(sent, 'space', 0, 0, tiled=True)  17.5 us
    all_to_all x2, starting transfers between devices, exchange(): swapped = lax.all_to_all(sent, 'space', 0, 0, tiled=True)  16.9 us
    pallas_call x1, Pallas kernels, input_spectrum(): pl.pallas_call(input_kernel, in_specs=[pl.BlockSpec(memory_space=pltpu.SM...  9.45 us
    pallas_call x1, Pallas kernels, gradient_spectrum(): pl.pallas_call(gradient_kernel, in_specs=[any_spec()] * 4, out_specs=[any...  7.04 us
    pallas_call x1, Pallas kernels, skip_term(): pl.pallas_call(skip_kernel, in_specs=[any_spec()] * 2 + in_vmem(3), out_s...  4.62 us
    pallas_call x1, Pallas kernels, backward(): pl.pallas_call(backward_kernel, in_specs=[vmem_spec(), any_spec(), vmem_s...  4.52 us
    pallas_call x1, Pallas kernels, middle(): pl.pallas_call(middle_kernel, in_specs=[pl.BlockSpec(memory_space=pltpu.S...  3.71 us
    ppermute x1, starting transfers between devices, body(): got = lax.ppermute(sent, 'dp', [(0, 1), (1, 0)])  3.37 us
  transfers between devices with their start and end apart: 3, of which 2 were waited for; matrix products, arithmetic and copies ran while one was open for 0% of the time, Pallas kernels for 26%

profile of v5, /device:TPU:1, one launch (start us, length us, event | category | flops | bytes accessed | tf_op | source)
XLA Modules:
  0.0 71.3 jit_solution(12328729349427267503)
XLA Ops:
  0.6 0.0 copy-start.1
  0.6 7.0 %gradient_spectrum.1 = (f32[64,16,128]{2,1,0:T(8,128)}, bf16[2048,1024]{1,0:T(8,128)(2,1)}) custom-call(f32[1,32,2,128,128]{4,3,2,1,0:T(8,128)} %pre_hbm.1, f32[1,32,2,128,128]{4,3,2,1,0:T(8,128)} %cot_hbm.1, bf16[1024,256]{1,0:T(8,128)(2,1)} %constant.22.clone.ztab_hbm, bf16[128,384]{1,0:T(8,128)(2,1)} %constant.23.clone.ytab_hbm), custom_call_target="tpu_custom_call" | custom-call | tf_op jit(solution)/shard_map/gradient_spectrum/pallas_call | solution.py:287
  7.7 10.4 %all-to-all-start = ((f32[64,16,128]{2,1,0:T(8,128)}), f32[64,16,128]{2,1,0:T(8,128)S(1)}, u32[]{:S(2)}, u32[]{:S(2)}) async-start(f32[64,16,128]{2,1,0:T(8,128)} %get-tuple-element.14), calls=%async_computation | async-start | bytes 1048576 | tf_op jit(solution)/shard_map/all_to_all | solution.py:718
  18.1 0.0 copy-done.1
  18.1 0.0 copy-start
  18.1 0.0 copy-start.2
  18.1 9.5 %input_spectrum.1 = (f32[64,24,128]{2,1,0:T(8,128)}, f32[16,16,2048]{2,1,0:T(8,128)S(1)}) custom-call(s32[1]{0:T(128)} %bitcast.one_ref.dp_ref, bf16[2048,1024]{1,0:T(8,128)(2,1)} %get-tuple-element.15.lhs_hbm, f32[1,32,2,128,128]{4,3,2,1,0:T(8,128)} %inp_hbm.1, bf16[1024,256]{1,0:T(8,128)(2,1)} %constant.22.clone.ztab_hbm, ...), custom_call_target="tpu_custom_call" | custom-call | tf_op jit(solution)/shard_map/input_spectrum/pallas_call | solution.py:389
  27.6 2.5 %all-to-all-done = f32[64,16,128]{2,1,0:T(8,128)S(1)} async-done(((f32[64,16,128]{2,1,0:T(8,128)}), f32[64,16,128]{2,1,0:T(8,128)S(1)}, u32[]{:S(2)}, u32[]{:S(2)}) %all-to-all-start) | async-done | bytes 524320 | tf_op jit(solution)/shard_map/all_to_all | solution.py:718
  30.0 0.0 copy-done
  30.0 0.0 copy-done.2
  30.0 0.0 copy-start.4
  30.0 0.0 copy-start.5
  30.0 3.7 %middle.1 = (f32[64,40,128]{2,1,0:T(8,128)}, f32[32,512]{1,0:T(8,128)S(1)}, f32[32,512]{1,0:T(8,128)S(1)}) custom-call(s32[1]{0:T(128)} %bitcast.one_ref.dp_ref, f32[1024,128]{1,0:T(8,128)S(1)} %bitcast.5, bf16[128,256]{1,0:T(8,128)(2,1)S(1)} %copy-done, bf16[256,192]{1,0:T(8,128)(2,1)S(1)} %copy-done.2, f32[16,16,2048]{2,1,0:T(8,128)S(1)} %get-tuple-element.16.early_ref, ...), custom_call_target="tpu_custom_call" | custom-call | tf_op jit(solution)/shard_map/middle/pallas_call | solution.py:547
  33.7 6.5 %all-to-all-start.1 = ((f32[64,40,128]{2,1,0:T(8,128)}), f32[64,40,128]{2,1,0:T(8,128)S(1)}, u32[]{:S(2)}, u32[]{:S(2)}) async-start(f32[64,40,128]{2,1,0:T(8,128)} %get-tuple-element.18), calls=%async_computation.1 | async-start | bytes 2621440 | tf_op jit(solution)/shard_map/all_to_all | solution.py:718
  40.3 0.0 copy-done.4
  40.3 0.0 copy-done.5
  40.3 4.6 %skip_term.1.term_hbm.after_hbm = f32[32,2,128,128]{3,2,1,0:T(8,128)} custom-call(bf16[2048,1024]{1,0:T(8,128)(2,1)} %get-tuple-element.15.lhs_hbm, f32[32,512]{1,0:T(8,128)S(1)} %get-tuple-element.19.after_hbm.grad_ref, f32[32,32]{1,0:T(8,128)S(1)} %copy-done.5, bf16[256,32]{1,0:T(8,128)(2,1)S(1)} %copy-done.4, bf16[256,32]{1,0:T(8,128)(2,1)S(1)} %copy-done.1), custom_call_target="tpu_custom_call" | custom-call | tf_op jit(solution)/shard_map/skip_term/pallas_call | solution.py:435
  44.9 0.0 copy-start.3
  44.9 15.0 %all-to-all-done.1 = f32[64,40,128]{2,1,0:T(8,128)S(1)} async-done(((f32[64,40,128]{2,1,0:T(8,128)}), f32[64,40,128]{2,1,0:T(8,128)S(1)}, u32[]{:S(2)}, u32[]{:S(2)}) %all-to-all-start.1) | async-done | bytes 1310752 | tf_op jit(solution)/shard_map/all_to_all | solution.py:718
  60.0 0.5 inputs_spectrum.1
  60.5 3.4 %collective-permute-start = (f32[72,512]{1,0:T(8,128)S(1)}, f32[72,512]{1,0:T(8,128)S(1)}, u32[]{:S(2)}, u32[]{:S(2)}) collective-permute-start(f32[72,512]{1,0:T(8,128)S(1)} %get-tuple-element.22.sent_ref), channel_id=1, source_target_pairs={{0,64},{64,0},{1,65},{65,1},{2,66},{66,2},{3,67},{67,3},{4,68},{68... | collective-permute-start | bytes 442376 | tf_op jit(solution)/shard_map/ppermute | solution.py:731
  63.8 0.0 copy-done.3
  63.8 4.5 %backward.1 = f32[1,32,2,128,128]{4,3,2,1,0:T(8,128)} custom-call(f32[2560,128]{1,0:T(8,128)S(1)} %bitcast.4, f32[32,2,128,128]{3,2,1,0:T(8,128)} %skip_term.1.term_hbm.after_hbm, bf16[128,384]{1,0:T(8,128)(2,1)S(1)} %copy-done.3, bf16[384,512]{1,0:T(8,128)(2,1)} %constant.28.clone.ztab_hbm), custom_call_target="tpu_custom_call" | custom-call | tf_op jit(solution)/shard_map/backward/pallas_call | solution.py:702
  68.4 0.0 collective-permute-done.got_ref
  68.4 2.7 %weight_gradient.1 = (f32[16,16,2048]{2,1,0:T(8,128)}, f32[32,32]{1,0:T(8,128)}) custom-call(f32[32,512]{1,0:T(8,128)S(1)} %get-tuple-element.19.after_hbm.grad_ref, f32[32,512]{1,0:T(8,128)S(1)} %get-tuple-element.21.field_ref, f32[72,512]{1,0:T(8,128)S(1)} %get-tuple-element.22.sent_ref, f32[72,512]{1,0:T(8,128)S(1)} %collective-permute-done.got_ref), custom_call_target="tpu_custom_call" | custom-call | tf_op jit(solution)/shard_map/weight_gradient/pallas_call | solution.py:635
Async XLA Ops:
  0.6 17.4 %copy-start.1 = (bf16[256,32]{1,0:T(8,128)(2,1)S(1)}, bf16[256,32]{1,0:T(8,128)(2,1)}, u32[]{:S(2)}) copy-start(bf16[256,32]{1,0:T(8,128)(2,1)} %constant.24.clone.fold_ref) | copy-start | bytes 49156
  7.7 22.3 %all-to-all-start = ((f32[64,16,128]{2,1,0:T(8,128)}), f32[64,16,128]{2,1,0:T(8,128)S(1)}, u32[]{:S(2)}, u32[]{:S(2)}) async-start(f32[64,16,128]{2,1,0:T(8,128)} %get-tuple-element.14), calls=%async_computation | async-start | bytes 1048576 | tf_op jit(solution)/shard_map/all_to_all | solution.py:718
  18.1 11.9 %copy-start = (bf16[128,256]{1,0:T(8,128)(2,1)S(1)}, bf16[128,256]{1,0:T(8,128)(2,1)}, u32[]{:S(2)}) copy-start(bf16[128,256]{1,0:T(8,128)(2,1)} %constant.25.clone.xtab_ref) | copy-start | bytes 196612
  18.1 11.9 %copy-start.2 = (bf16[256,192]{1,0:T(8,128)(2,1)S(1)}, bf16[256,192]{1,0:T(8,128)(2,1)}, u32[]{:S(2)}) copy-start(bf16[256,192]{1,0:T(8,128)(2,1)} %constant.26.clone.back_ref) | copy-start | bytes 294916
  30.0 10.3 %copy-start.4 = (bf16[256,32]{1,0:T(8,128)(2,1)S(1)}, bf16[256,32]{1,0:T(8,128)(2,1)}, u32[]{:S(2)}) copy-start(bf16[256,32]{1,0:T(8,128)(2,1)} %constant.27.clone.rows_ref) | copy-start | bytes 49156
  30.0 10.3 %copy-start.5 = (f32[32,32]{1,0:T(8,128)S(1)}, f32[32,32]{1,0:T(8,128)}, u32[]{:S(2)}) copy-start(f32[32,32]{1,0:T(8,128)} %skip_ref.1) | copy-start | bytes 12292
  33.7 26.2 %all-to-all-start.1 = ((f32[64,40,128]{2,1,0:T(8,128)}), f32[64,40,128]{2,1,0:T(8,128)S(1)}, u32[]{:S(2)}, u32[]{:S(2)}) async-start(f32[64,40,128]{2,1,0:T(8,128)} %get-tuple-element.18), calls=%async_computation.1 | async-start | bytes 2621440 | tf_op jit(solution)/shard_map/all_to_all | solution.py:718
  44.9 18.9 %copy-start.3 = (bf16[128,384]{1,0:T(8,128)(2,1)S(1)}, bf16[128,384]{1,0:T(8,128)(2,1)}, u32[]{:S(2)}) copy-start(bf16[128,384]{1,0:T(8,128)(2,1)} %constant.29.clone.ytab_ref) | copy-start | bytes 294916
  60.5 7.9 %collective-permute-start = (f32[72,512]{1,0:T(8,128)S(1)}, f32[72,512]{1,0:T(8,128)S(1)}, u32[]{:S(2)}, u32[]{:S(2)}) collective-permute-start(f32[72,512]{1,0:T(8,128)S(1)} %get-tuple-element.22.sent_ref), channel_id=1, source_target_pairs={{0,64},{64,0},{1,65},{65,1},{2,66},{66,2},{3,67},{67,3},{4,68},{68... | collective-permute-start | bytes 442376 | tf_op jit(solution)/shard_map/ppermute | solution.py:731
